TPU v7x, 256 devices: a whole 4x4x8 slice. The times are simulated.
256 devices in a mesh: segment: 16 (over z_lo, y), seq: 16 (over z_hi, x, core).
Axes of the slice: x: 4, y: 4, z: 8 (z_hi: 2, z_lo: 4; z = z_hi * 4 + z_lo), core: 2. Of those that a mesh axis runs over, the one named last changes fastest.
Arguments:
- queue: bfloat16 [16, 2048, 3072], P('segment', 'seq'), may hold values from -4 to 4
- fresh_noise: bfloat16 [2048, 3072], P('seq'), may hold values from -6 to 6
- w_mod: bfloat16 [16, 3072, 9216], P('segment', None, 'seq'), may hold values from -0.109375 to 0.109375
- w_qkv: bfloat16 [16, 3072, 16, 384], P('segment', None, 'seq'), may hold values from -0.109375 to 0.109375
- w_out: bfloat16 [16, 2048, 3072], P('segment', 'seq'), may hold values from -0.125 to 0.125
- q_gain: float32 [16, 128], P('segment'), may hold values from 1.5 to 7, as said below
- k_gain: float32 [16, 128], P('segment'), may hold values from 1.5 to 7, as said below
- levels: int32 [16], P('segment'), may hold values from 0 to 49
- plan: int32 [50], replicated, may hold values from 0 to 999
- positions: int32 [16], P('segment'), may hold values from 0 to 1023
Outputs:
- queue_next: bfloat16 [16, 2048, 3072], P('segment', 'seq')
- clean_frame: bfloat16 [2048, 3072], P('seq', 'segment')
Inputs may be any that keep to these rules, and one draw needn't show every extreme that they name: `q_gain`: query gains are positive. `k_gain`: key gains are positive.
All inputs are finite; a program needn't handle non-finite values.
Results may differ from a plain program's by a relative error of at most 0.035.
Values may be sent and summed in bfloat16 or wider, within the bound.
No kernel may reach another device: no remote copies, remote signals or barrier semaphores. Data moves between devices by JAX's collectives and lax.ppermute only.
A program may use at most 128 MiB of HBM per device.

v0:
```python
import functools
import math

import jax
import jax.numpy as jnp
import numpy as np
from jax import lax
from jax.experimental import pallas as pl
from jax.experimental.pallas import tpu as pltpu
from jax.sharding import PartitionSpec as P

GRID_W = 32
EPSILON = 1e-06
ROPE_BASE = 256.0
HEAD = 128
NEG = -1e30
XN, CN, ZN = 4, 2, 2
VMEM = pl.BlockSpec(memory_space=pltpu.VMEM)
SMEM = pl.BlockSpec(memory_space=pltpu.SMEM)
LIMIT = 32 << 20


def seq_id(z, x, c):
    return (z % ZN) * XN * CN + (x % XN) * CN + (c % CN)


ALL = [(z, x, c) for z in range(ZN) for x in range(XN) for c in range(CN)]
X_UP = [(seq_id(z, x, c), seq_id(z, x + 1, c)) for z, x, c in ALL]
X_DOWN = [(seq_id(z, x, c), seq_id(z, x - 1, c)) for z, x, c in ALL]
X_FAR = [(seq_id(z, x, c), seq_id(z, x + 2, c)) for z, x, c in ALL]
X_PAIR = [(seq_id(z, x, c), seq_id(z, x ^ 1, c)) for z, x, c in ALL]
Z_SWAP = [(seq_id(z, x, c), seq_id(z + 1, x, c)) for z, x, c in ALL]
C_SWAP = [(seq_id(z, x, c), seq_id(z, x, c + 1)) for z, x, c in ALL]


def on_seq(value, pairs):
    return lax.ppermute(value, "seq", pairs)


def tie(*values):
    return lax.optimization_barrier(values)


def lane_order():
    time_dim = HEAD // 8
    space_dim = (HEAD - time_dim) // 2
    first, second, start = [], [], 0
    for section in (time_dim, space_dim, space_dim):
        half = section // 2
        first += list(range(start, start + half))
        second += list(range(start + half, start + section))
        start += section
    return np.array(first + second)


ORDER = lane_order()


def order_matrix():
    one = np.zeros((3 * HEAD, 3 * HEAD), np.float32)
    for part in range(2):
        one[part * HEAD + ORDER, part * HEAD + np.arange(HEAD)] = 1.0
    one[2 * HEAD + np.arange(HEAD), 2 * HEAD + np.arange(HEAD)] = 1.0
    return one


def time_embedding(step_values, width):
    half_width = width // 2
    counter = jnp.arange(half_width, dtype=jnp.float32)
    frequency = jnp.exp(-jnp.log(10000.0) * counter / half_width)
    angles = step_values.astype(jnp.float32)[:, None] * frequency[None, :]
    return jnp.concatenate([jnp.cos(angles), jnp.sin(angles)], axis=-1)


def rope_frequencies():
    time_dim = HEAD // 8
    space_dim = (HEAD - time_dim) // 2
    lanes = np.zeros((3, HEAD), np.float32)
    start = 0
    for at, section in enumerate((time_dim, space_dim, space_dim)):
        half = section // 2
        power = np.float32(ROPE_BASE) ** (np.float32(-2.0) * np.arange(half, dtype=np.float32) / np.float32(section))
        lanes[at, start : start + half] = power
        lanes[at, HEAD // 2 + start : HEAD // 2 + start + half] = power
        start += half
    return lanes


def rope_tables(position, places, tok_dev):
    lanes = jnp.asarray(rope_frequencies())
    sign = jnp.where(jnp.arange(HEAD) < HEAD // 2, -1.0, 1.0)
    rows = tok_dev // GRID_W
    grid_row = (jnp.stack(places)[:, None] * rows + jnp.arange(rows, dtype=jnp.int32)).astype(jnp.float32)
    grid_col = jnp.arange(GRID_W, dtype=jnp.int32).astype(jnp.float32)
    by_row = position.astype(jnp.float32) * lanes[0] + grid_row[..., None] * lanes[1]
    by_col = grid_col[:, None] * lanes[2]
    column = lanes[2] > 0
    tables = []
    for turn, factor in ((jnp.cos, 1.0), (jnp.sin, sign)):
        table = jnp.where(column, (turn(by_col) * factor)[None, None], (turn(by_row) * factor)[:, :, None])
        tables.append(table.reshape(-1, HEAD))
    return tuple(tables)


def norm_kernel(x_ref, o_ref):
    x = x_ref[...].astype(jnp.float32)
    centre = jnp.mean(x, axis=-1, keepdims=True)
    x = x - centre
    spread = jnp.mean(x * x, axis=-1, keepdims=True)
    o_ref[...] = (x * lax.rsqrt(spread + EPSILON)).astype(jnp.bfloat16)


def norm_rows(x):
    rows, width = x.shape
    block = 64
    return pl.pallas_call(
        norm_kernel,
        grid=(rows // block,),
        in_specs=[pl.BlockSpec((block, width), lambda i: (i, 0))],
        out_specs=pl.BlockSpec((block, width), lambda i: (i, 0)),
        out_shape=jax.ShapeDtypeStruct(x.shape, jnp.bfloat16),
        cost_estimate=pl.CostEstimate(flops=1, bytes_accessed=1, transcendentals=0),
        name="norm_rows",
    )(x)


def qkv_kernel(count, scale_ref, shift_ref, cos_ref, sin_ref, gq_ref, gk_ref, w_mine, w_other, *refs):
    x_refs = refs[:count]
    q_mine, kv_mine, all_other, acc = refs[count:]
    step = pl.program_id(0)
    x = jnp.concatenate([r[...] for r in x_refs], axis=0).astype(jnp.float32)
    x = (x * scale_ref[...] + shift_ref[...]).astype(jnp.bfloat16)
    w = jnp.concatenate([w_mine[...], w_other[...]], axis=1)
    part = jnp.dot(x, w, preferred_element_type=jnp.float32)

    @pl.when(step == 0)
    def _():
        acc[...] = part

    @pl.when(step > 0)
    def _():
        acc[...] += part

    @pl.when(step == pl.num_programs(0) - 1)
    def _():
        cos, sin = cos_ref[...], sin_ref[...]

        def turned(y, gain):
            y = y * lax.rsqrt(jnp.mean(y * y, axis=-1, keepdims=True) + EPSILON) * gain
            return (y * cos + pltpu.roll(y, HEAD // 2, 1) * sin).astype(jnp.bfloat16)

        q_mine[...] = turned(acc[:, :HEAD], gq_ref[...])
        kv_mine[:, :HEAD] = turned(acc[:, HEAD : 2 * HEAD], gk_ref[...])
        kv_mine[:, HEAD:] = acc[:, 2 * HEAD : 3 * HEAD].astype(jnp.bfloat16)
        all_other[:, :HEAD] = turned(acc[:, 3 * HEAD : 4 * HEAD], gq_ref[...])
        all_other[:, HEAD : 2 * HEAD] = turned(acc[:, 4 * HEAD : 5 * HEAD], gk_ref[...])
        all_other[:, 2 * HEAD :] = acc[:, 5 * HEAD :].astype(jnp.bfloat16)


def qkv(limit, blocks, scale, shift, cos, sin, gq, gk, w_mine, w_other):
    width = w_mine.shape[0]
    rows = sum(b.shape[0] for b in blocks)
    depth = 1536
    row_spec = pl.BlockSpec((1, depth), lambda k: (0, k))
    whole = lambda a: pl.BlockSpec(a.shape, lambda k: (0, 0))
    w_spec = pl.BlockSpec((depth, 3 * HEAD), lambda k: (k, 0))
    out = [jax.ShapeDtypeStruct((rows, n), jnp.bfloat16) for n in (HEAD, 2 * HEAD, 3 * HEAD)]
    return pl.pallas_call(
        functools.partial(qkv_kernel, len(blocks)),
        grid=(width // depth,),
        in_specs=[row_spec, row_spec, whole(cos), whole(sin), whole(gq), whole(gk), w_spec, w_spec]
        + [pl.BlockSpec((b.shape[0], depth), lambda k: (0, k)) for b in blocks],
        out_specs=[pl.BlockSpec(o.shape, lambda k: (0, 0)) for o in out],
        out_shape=out,
        scratch_shapes=[pltpu.VMEM((rows, 6 * HEAD), jnp.float32)],
        compiler_params=pltpu.CompilerParams(vmem_limit_bytes=limit),
        cost_estimate=pl.CostEstimate(flops=1, bytes_accessed=1, transcendentals=0),
        name="qkv",
    )(scale, shift, cos, sin, gq, gk, w_mine, w_other, *blocks)


def attend_kernel(flag_ref, *refs):
    q_in, kv_in, o_refs = refs[:4], refs[4:10], refs[10:12]
    q_a, q_b, kv_all, sems = refs[12:]
    kv_refs = [kv_all.at[i] for i in range(6)]
    copies = [pltpu.make_async_copy(q_in[i], (q_a, q_b)[i % 2].at[i // 2], sems.at[6 + i]) for i in range(4)]
    copies += [pltpu.make_async_copy(kv_in[i], kv_refs[i], sems.at[i]) for i in range(6)]
    for copy in copies:
        copy.start()
    for copy in copies[:4]:
        copy.wait()
    blocks = q_a.shape[1] // HEAD
    chunk = 512
    per = kv_all.shape[1] // chunk
    state = [(None, None)] * 4
    for group in range(3):
        flag = None if group == 0 else flag_ref[group - 1] > 0
        parts = [(kv_refs[2 * group + i], j * chunk) for i in range(2) for j in range(per)]
        for copy in copies[4 + 2 * group : 6 + 2 * group]:
            copy.wait()
        for at, q_ref in enumerate((q_a.at[0], q_b.at[0], q_a.at[1], q_b.at[1])):
            q = q_ref[:, :HEAD]
            acc, m = state[at]
            scores = [
                lax.dot_general(
                    q,
                    ref[row : row + chunk, :HEAD],
                    (((1,), (1,)), ((), ())),
                    preferred_element_type=jnp.float32,
                )
                for ref, row in parts
            ]
            top = functools.reduce(jnp.maximum, [jnp.max(s, axis=1, keepdims=True) for s in scores])
            if flag is not None:
                top = jnp.where(flag, top, NEG)
            later = top if m is None else jnp.maximum(m, top)
            less = later if flag is None else jnp.where(flag, later, -NEG)
            total = None
            for score, (ref, row) in zip(scores, parts):
                p = jnp.exp2(score - less).astype(jnp.bfloat16)
                v = ref[row : row + chunk, HEAD:]
                v = jnp.concatenate([v, jnp.ones_like(v)], axis=1)
                d = jnp.dot(p, v, preferred_element_type=jnp.float32)
                total = d if total is None else total + d
            acc = total if acc is None else acc * jnp.exp2(m - later) + total
            state[at] = (acc, later)
    for at, (acc, _) in enumerate(state):
        o = (acc[:, :HEAD] / acc[:, HEAD:]).astype(jnp.bfloat16)
        for block in range(blocks):
            row = (2 * block + at % 2) * HEAD
            o_refs[at // 2][row : row + HEAD, :] = o[block * HEAD : (block + 1) * HEAD]


def attend(flags, queries, key_values):
    rows = 2 * queries[0].shape[0]
    return pl.pallas_call(
        attend_kernel,
        in_specs=[SMEM] + [pl.BlockSpec(memory_space=pl.ANY)] * (4 + len(key_values)),
        out_specs=[VMEM] * 2,
        out_shape=[jax.ShapeDtypeStruct((rows, HEAD), jnp.bfloat16)] * 2,
        scratch_shapes=[
            pltpu.VMEM((2, *queries[0].shape), jnp.bfloat16),
            pltpu.VMEM((2, *queries[1].shape), jnp.bfloat16),
            pltpu.VMEM((len(key_values), *key_values[0].shape), jnp.bfloat16),
            pltpu.SemaphoreType.DMA((4 + len(key_values),)),
        ],
        compiler_params=pltpu.CompilerParams(vmem_limit_bytes=60 << 20),
        cost_estimate=pl.CostEstimate(flops=1, bytes_accessed=1, transcendentals=0),
        name="attend",
    )(flags, *queries, *key_values)


def pair_kernel(near_ref, far_ref, *outs):
    rows = outs[0].shape[0]
    for at, out in enumerate(outs):
        out[:, :HEAD] = near_ref[at * rows : (at + 1) * rows, :]
        out[:, HEAD:] = far_ref[at * rows : (at + 1) * rows, :]


def pair_heads(near, far):
    rows = near.shape[0] // XN
    return pl.pallas_call(
        pair_kernel,
        in_specs=[VMEM] * 2,
        out_specs=[VMEM] * XN,
        out_shape=[jax.ShapeDtypeStruct((rows, 2 * HEAD), jnp.bfloat16)] * XN,
        cost_estimate=pl.CostEstimate(flops=1, bytes_accessed=1, transcendentals=0),
        name="pair_heads",
    )(near, far)


def out_kernel(count, *refs):
    a_refs = refs[:4]
    w_refs = refs[4 : 4 + count]
    mine, other = refs[4 + count :]
    a = jnp.concatenate([r[...] for r in a_refs], axis=1)
    w = jnp.concatenate([r[...] for r in w_refs], axis=0)
    part = jnp.dot(a, w, preferred_element_type=jnp.float32)
    rows = mine.shape[0]
    mine[...] = part[:rows]
    other[...] = part[rows:].astype(jnp.bfloat16)


def out_project(a_parts, w_parts):
    rows = a_parts[0].shape[0] // 2
    width = w_parts[0].shape[1]
    depth = sum(w.shape[0] for w in w_parts)
    step = 512
    return pl.pallas_call(
        functools.partial(out_kernel, len(w_parts)),
        grid=(width // step,),
        in_specs=[pl.BlockSpec(a.shape, lambda n: (0, 0)) for a in a_parts]
        + [pl.BlockSpec((w.shape[0], step), lambda n: (0, n)) for w in w_parts],
        out_specs=[pl.BlockSpec((rows, step), lambda n: (0, n))] * 2,
        out_shape=[
            jax.ShapeDtypeStruct((rows, width), jnp.float32),
            jax.ShapeDtypeStruct((rows, width), jnp.bfloat16),
        ],
        compiler_params=pltpu.CompilerParams(vmem_limit_bytes=60 << 20),
        cost_estimate=pl.CostEstimate(flops=1, bytes_accessed=1, transcendentals=0),
        name="out_project",
    )(*a_parts, *w_parts)


def gather_step(part, pairs, bit):
    got = on_seq(part, pairs)
    return jnp.concatenate([jnp.where(bit == 0, part, got), jnp.where(bit == 0, got, part)], axis=0)


def finish_kernel(side_n, queue_ref, gate_ref, mine_ref, got_ref, sent_ref, *pieces):
    width = queue_ref.shape[1]
    columns = width // (side_n * side_n)
    projected = mine_ref[...] + got_ref[...].astype(jnp.float32)
    finished = (queue_ref[...].astype(jnp.float32) + gate_ref[...] * projected).astype(jnp.bfloat16)
    for place, piece in enumerate(pieces):
        for row in range(side_n):
            at = (row * side_n + place) * columns
            piece[:, row * columns : (row + 1) * columns] = finished[:, at : at + columns]
    sent_ref[...] = finished


def finish(side_n, queue, gate, mine, got):
    rows, width = queue.shape
    step = 32
    spec = lambda n: pl.BlockSpec((step, n), lambda i: (i, 0))
    out = [jax.ShapeDtypeStruct((rows, width), jnp.bfloat16)]
    out += [jax.ShapeDtypeStruct((rows, width // side_n), jnp.bfloat16)] * side_n
    return pl.pallas_call(
        functools.partial(finish_kernel, side_n),
        grid=(rows // step,),
        in_specs=[spec(width), pl.BlockSpec((1, width), lambda i: (0, 0)), spec(width), spec(width)],
        out_specs=[spec(o.shape[1]) for o in out],
        out_shape=out,
        compiler_params=pltpu.CompilerParams(vmem_limit_bytes=60 << 20),
        cost_estimate=pl.CostEstimate(flops=1, bytes_accessed=1, transcendentals=0),
        name="finish",
    )(queue, gate, mine, got)


def shards(queue, fresh_noise, w_mod, w_qkv, w_out, q_gain, k_gain, levels, plan, positions):
    segments = lax.axis_size("segment")
    segment_at = lax.axis_index("segment")
    seq_at = lax.axis_index("seq")
    z, x, c = seq_at // (XN * CN), (seq_at // CN) % XN, seq_at % CN
    tok_dev, width = queue.shape[1], queue.shape[2]
    up = [(i, (i + 1) % segments) for i in range(segments)]
    down = [((i + 1) % segments, i) for i in range(segments)]

    half = tok_dev // 2
    one_hot = order_matrix()
    order = jnp.asarray(one_hot, jnp.bfloat16)

    def ordered(w):
        return jnp.dot(w, order, preferred_element_type=jnp.float32).astype(jnp.bfloat16)

    def table(zz, position):
        places = [zz * XN * CN + ((x + r) % XN) * CN + c for r in (0, XN - 1, 1, 2)]
        return rope_tables(position, places, tok_dev)

    w_raw = w_qkv[0].reshape(width, 3 * HEAD)
    w_out_own = w_out[0]
    w_got = on_seq(w_raw, C_SWAP)
    normed = norm_rows(queue[0])
    z_normed, below, above = on_seq(normed, Z_SWAP), on_seq(normed, X_UP), on_seq(normed, X_DOWN)

    levels, normed = tie(levels, normed)
    picked = levels[:, None] == jnp.arange(plan.shape[0], dtype=jnp.int32)[None, :]
    step_values = jnp.sum(jnp.where(picked, plan[None, :], 0), axis=1)
    embedding = jax.nn.silu(time_embedding(step_values, width)).astype(jnp.bfloat16)
    mod = jnp.dot(embedding, w_mod[0], preferred_element_type=jnp.float32)
    mod, w_raw = tie(mod, w_raw)
    w_mine = ordered(w_raw)
    mod = gather_step(mod, C_SWAP, c)
    mod, w_mine, below, above, positions = tie(mod, w_mine, below, above, positions)
    top, low = below[:half], above[half:]
    mod = gather_step(mod, X_PAIR, x % 2)
    mod, top, low, positions = tie(mod, top, low, positions)
    far_top, far_low = on_seq(top, X_UP), on_seq(low, X_DOWN)
    near_table = table(z, positions[0])
    mod = gather_step(mod, X_FAR, x // 2)
    mod, w_got, positions, *near_table = tie(mod, w_got, positions, *near_table)
    w_other = ordered(w_got)
    mod = gather_step(mod, Z_SWAP, z)
    gains = jnp.sum(jnp.concatenate([q_gain, k_gain])[:, :, None] * jnp.asarray(one_hot[None, :HEAD, :HEAD]), axis=1)
    gq = gains[:1] * (HEAD**-0.5 * math.log2(math.e))
    gk = gains[1:]
    z_normed, far_top, far_low, w_out_own, positions, gq, gk = tie(
        z_normed, far_top, far_low, w_out_own, positions, gq, gk
    )
    z_below, z_above = on_seq(z_normed, X_UP), on_seq(z_normed, X_DOWN)
    w_far = on_seq(w_out_own, Z_SWAP)
    far_table = table(1 - z, positions[0])
    modulation = mod.reshape(1, -1)
    shift_row = modulation[:, :width]
    scale_row = 1.0 + modulation[:, width : 2 * width]
    gate_row = modulation[:, 2 * width :]

    def half_frame(limit, blocks, tables):
        return qkv(limit, blocks, scale_row, shift_row, *tables, gq, gk, w_mine, w_other)

    def with_partner(q_mine, kv_mine, other):
        got = on_seq(other, C_SWAP)
        return (q_mine, got), jnp.concatenate([kv_mine, got[:, HEAD:]], axis=0)

    def halo(kv):
        return lax.ppermute(kv, "segment", up), lax.ppermute(kv, "segment", down)

    near_half = half_frame(60 << 20, (normed, below, above, far_top, far_low), near_table)
    z_below, z_above, *near_half = tie(z_below, z_above, *near_half)
    top, low = z_below[:half], z_above[half:]
    top, low, w_out_own, *near_half = tie(top, low, w_out_own, *near_half)
    w_below, w_above = on_seq(w_out_own, X_UP), on_seq(w_out_own, X_DOWN)
    z_far_top, z_far_low = on_seq(top, X_UP), on_seq(low, X_DOWN)
    q_near, kv_near = with_partner(*near_half)
    halo_near = halo(kv_near)
    z_normed, z_far_top, kv_near, w_far = tie(z_normed, z_far_top, kv_near, w_far)
    far_half = half_frame(LIMIT, (z_normed, z_below, z_above, z_far_top, z_far_low), far_table)
    q_far, kv_far = with_partner(*far_half)
    kv_far, *halo_near = tie(kv_far, *halo_near)
    halo_far = halo(kv_far)
    kv_far, w_below, w_above = tie(kv_far, w_below, w_above)
    top, low = w_below[:half], w_above[half:]
    top, low, w_far, *halo_far = tie(top, low, w_far, *halo_far)
    near_w = [w_out_own, w_below, w_above, on_seq(top, X_UP), on_seq(low, X_DOWN)]

    flags = jnp.stack([segment_at > 0, segment_at < segments - 1]).astype(jnp.int32)
    w_below, w_above = on_seq(w_far, X_UP), on_seq(w_far, X_DOWN)
    key_values = (kv_near, kv_far, halo_near[0], halo_far[0], halo_near[1], halo_far[1])
    near, theirs = attend(flags, (*q_near, *q_far), key_values)
    far = on_seq(theirs, Z_SWAP)
    near, w_below, w_above = tie(near, w_below, w_above)
    top, low = w_below[:half], w_above[half:]
    near, top, low = tie(near, top, low)
    far_w = [w_far, w_below, w_above, on_seq(top, X_UP), on_seq(low, X_DOWN)]
    sides = pair_heads(near, far)
    a_parts = [sides[0], on_seq(sides[2], X_UP), on_seq(sides[1], X_DOWN), on_seq(sides[3], X_FAR)]
    w_parts = []
    for at in range(4):
        for block in (near_w, far_w):
            w_parts += block[at : at + 1] if at < 3 else block[3:5]
    mine, other = out_project(a_parts, w_parts)
    side_n = 4
    last = segments - 1
    finished, *pieces = finish(side_n, queue[0], gate_row, mine, on_seq(other, C_SWAP))
    arrived = lax.ppermute(finished, "segment", up[:-1])
    queue_next = jnp.where(segment_at == 0, fresh_noise, arrived)[None]

    columns = width // segments
    spread = jnp.where(segment_at == last, pieces[-1], jnp.zeros((), jnp.bfloat16))
    for place in range(side_n - 1):
        spread += lax.ppermute(pieces[place], "segment", [(last, last - (side_n - 1) + place)])
    clean = jnp.where(segment_at >= segments - side_n, spread[:, (side_n - 1) * columns :], jnp.zeros((), jnp.bfloat16))
    for row in range(side_n - 1):
        clean += lax.ppermute(
            spread[:, row * columns : (row + 1) * columns],
            "segment",
            [(segments - side_n + place, row * side_n + place) for place in range(side_n)],
        )
    return (queue_next, clean)


def solution(mesh):
    placed = (
        P("segment", "seq", None),
        P("seq", None),
        P("segment", None, "seq"),
        P("segment", None, "seq", None),
        P("segment", "seq", None),
        P("segment", None),
        P("segment", None),
        P("segment"),
        P(),
        P("segment"),
    )
    return jax.shard_map(
        shards,
        mesh=mesh,
        in_specs=placed,
        out_specs=(P("segment", "seq", None), P("seq", "segment")),
        check_vma=False,
    )
```

profile of v0, /device:TPU:64, one launch (start us, length us, event | category | flops | bytes accessed | tf_op | source)
XLA Modules:
  0.0 242.8 jit_solution(17537495007308614814)
XLA Ops:
  0.7 2.6 %norm_rows.1.refs_0_ = bf16[128,3072]{1,0:T(8,128)(2,1)} custom-call(bf16[128,3072]{1,0:T(8,128)(2,1)} %bitcast.47), custom_call_target="tpu_custom_call" | custom-call | flops 1 | bytes 1 | tf_op jit(solution)/shard_map/norm_rows/pallas_call | solution.py:116
  4.7 1.7 collective-permute-start.2
  6.5 5.4 %collective-permute-start.7 = (bf16[128,3072]{1,0:T(8,128)(2,1)}, bf16[128,3072]{1,0:T(8,128)(2,1)}, u32[]{:S(2)}, u32[]{:S(2)}) collective-permute-start(bf16[128,3072]{1,0:T(8,128)(2,1)} %norm_rows.1.refs_0_), channel_id=1, source_target_pairs={{0,8},{1,9},{2,10},{3,11},{4,12},{5,13},{6,14},{7,15},{8,0},{9,1},... | collective-permute-start | bytes 2359304 | tf_op jit(solution)/shard_map/ppermute | solution.py:37
  14.6 1.6 fusion
  20.4 4.7 %convolution_convert_fusion.1.w_mine = bf16[3072,384]{1,0:T(8,128)(2,1)} fusion(bf16[3072,384]{1,0:T(8,128)(2,1)} %bitcast.46, bf16[384,384]{1,0:T(8,128)(2,1)} %constant.127.clone), kind=kOutput, calls=%fused_computation.1 | convolution fusion | flops 907149312 | bytes 5013504 | tf_op jit(solution)/shard_map/dot_general | solution.py:354
  28.7 1.8 slice.77
  30.5 1.8 slice.78
  33.6 2.7 %collective-permute-start.4 = (f32[4,576]{1,0:T(4,128)}, f32[4,576]{1,0:T(4,128)}, u32[]{:S(2)}, u32[]{:S(2)}) collective-permute-start(f32[4,576]{1,0:T(4,128)} %pad_maximum_fusion.5), channel_id=1, source_target_pairs={{0,4},{1,5},{2,6},{3,7},{4,0},{5,1},{6,2},{7,3},{8,12},{9,13},{10,... | collective-permute-start | bytes 27656 | tf_op jit(solution)/shard_map/ppermute | solution.py:37
  36.5 3.0 %collective-permute-start.9 = (bf16[64,3072]{1,0:T(8,128)(2,1)}, bf16[64,3072]{1,0:T(8,128)(2,1)}, u32[]{:S(2)}, u32[]{:S(2)}) collective-permute-start(bf16[64,3072]{1,0:T(8,128)(2,1)} %slice.78), channel_id=1, source_target_pairs={{0,6},{1,7},{2,0},{3,1},{4,2},{5,3},{6,4},{7,5},{8,14},{9,15},{10,... | collective-permute-start | bytes 1179656 | tf_op jit(solution)/shard_map/ppermute | solution.py:37
  40.2 1.6 bitcast_select_fusion.1
  42.6 3.8 %collective-permute-done.7.refs_0_ = bf16[128,3072]{1,0:T(8,128)(2,1)} collective-permute-done((bf16[128,3072]{1,0:T(8,128)(2,1)}, bf16[128,3072]{1,0:T(8,128)(2,1)}, u32[]{:S(2)}, u32[]{:S(2)}) %collective-permute-start.7) | collective-permute-done | bytes 786464 | tf_op jit(solution)/shard_map/ppermute | solution.py:37
  46.3 2.0 collective-permute-done.8.refs_3_
  48.4 3.2 %collective-permute-start.11 = (bf16[128,3072]{1,0:T(8,128)(2,1)}, bf16[128,3072]{1,0:T(8,128)(2,1)}, u32[]{:S(2)}, u32[]{:S(2)}) collective-permute-start(bf16[128,3072]{1,0:T(8,128)(2,1)} %collective-permute-done.7.refs_0_), channel_id=1, source_target_pairs={{0,6},{1,7},{2,0},{3,1},{4,2},{5,3},{6,4},{7,5},{8,14},{9,15},{10,... | collective-permute-start | bytes 2359304 | tf_op jit(solution)/shard_map/ppermute | solution.py:37
  51.6 14.6 %collective-permute-start.6 = (f32[8,576]{1,0:T(8,128)S(1)}, f32[8,576]{1,0:T(8,128)S(1)}, u32[]{:S(2)}, u32[]{:S(2)}) collective-permute-start(f32[8,576]{1,0:T(8,128)S(1)} %pad_maximum_fusion.3), channel_id=1, source_target_pairs={{0,8},{1,9},{2,10},{3,11},{4,12},{5,13},{6,14},{7,15},{8,0},{9,1},... | collective-permute-start | bytes 55304 | tf_op jit(solution)/shard_map/ppermute | solution.py:37
  66.3 4.7 %convolution_convert_fusion.w_other = bf16[3072,384]{1,0:T(8,128)(2,1)} fusion(bf16[3072,384]{1,0:T(8,128)(2,1)} %collective-permute-done.5, bf16[384,384]{1,0:T(8,128)(2,1)} %constant.127.clone), kind=kOutput, calls=%fused_computation | convolution fusion | flops 907149312 | bytes 5013504 | tf_op jit(solution)/shard_map/dot_general | solution.py:354
  70.9 2.9 %collective-permute-start.14 = (bf16[128,3072]{1,0:T(8,128)(2,1)}, bf16[128,3072]{1,0:T(8,128)(2,1)}, u32[]{:S(2)}, u32[]{:S(2)}) collective-permute-start(bf16[128,3072]{1,0:T(8,128)(2,1)} %bitcast.16.refs_4_), channel_id=1, source_target_pairs={{0,8},{1,9},{2,10},{3,11},{4,12},{5,13},{6,14},{7,15},{8,0},{9,1},... | collective-permute-start | bytes 2359304 | tf_op jit(solution)/shard_map/ppermute | solution.py:37
  77.3 7.5 %qkv.2 = (bf16[512,128]{1,0:T(8,128)(2,1)}, bf16[512,256]{1,0:T(8,128)(2,1)}, bf16[512,384]{1,0:T(8,128)(2,1)}) custom-call(f32[1,3072]{1,0:T(1,128)} %get-tuple-element.164.scale_ref, f32[1,3072]{1,0:T(1,128)} %get-tuple-element.163.shift_ref, f32[512,128]{1,0:T(8,128)} %get-tuple-element.92.cos_ref, f32[512,128]{1,0:T(8,128)} %get-tuple-element.93.sin_ref, ...), custom_call_target="tpu_custom_call" | custom-call | flops 1 | bytes 1 | tf_op jit(solution)/shard_map/qkv/pallas_call | solution.py:168
  87.4 3.2 %collective-permute-start.15 = (bf16[64,3072]{1,0:T(8,128)(2,1)S(1)}, bf16[64,3072]{1,0:T(8,128)(2,1)S(1)}, u32[]{:S(2)}, u32[]{:S(2)}) collective-permute-start(bf16[64,3072]{1,0:T(8,128)(2,1)S(1)} %slice.88), channel_id=1, source_target_pairs={{0,6},{1,7},{2,0},{3,1},{4,2},{5,3},{6,4},{7,5},{8,14},{9,15},{10,... | collective-permute-start | bytes 1179656 | tf_op jit(solution)/shard_map/ppermute | solution.py:37
  92.4 1.7 collective-permute-start.17
  94.1 2.6 %collective-permute-start.18 = (bf16[1024,256]{1,0:T(8,128)(2,1)S(1)}, bf16[1024,256]{1,0:T(8,128)(2,1)S(1)}, u32[]{:S(2)}, u32[]{:S(2)}) collective-permute-start(bf16[1024,256]{1,0:T(8,128)(2,1)S(1)} %pad_maximum_fusion.refs_4_), channel_id=1, source_target_pairs={{16,0},{32,16},{48,32},{64,48},{80,64},{96,80},{112,96},{128,112},... | collective-permute-start | bytes 1572872 | tf_op jit(solution)/shard_map/ppermute | solution.py:406
  96.8 11.5 %collective-permute-done.14.refs_5_ = bf16[128,3072]{1,0:T(8,128)(2,1)} collective-permute-done((bf16[128,3072]{1,0:T(8,128)(2,1)}, bf16[128,3072]{1,0:T(8,128)(2,1)}, u32[]{:S(2)}, u32[]{:S(2)}) %collective-permute-start.14) | collective-permute-done | bytes 786464 | tf_op jit(solution)/shard_map/ppermute | solution.py:37
  108.4 1.7 copy-done.2
  110.0 5.1 %qkv.3 = (bf16[512,128]{1,0:T(8,128)(2,1)S(1)}, bf16[512,256]{1,0:T(8,128)(2,1)S(1)}, bf16[512,384]{1,0:T(8,128)(2,1)S(1)}) custom-call(f32[1,3072]{1,0:T(1,128)S(1)} %copy-done.5, f32[1,3072]{1,0:T(1,128)S(1)} %copy-done.4, f32[512,128]{1,0:T(8,128)S(1)} %get-tuple-element.181.cos_ref, f32[512,128]{1,0:T(8,128)S(1)} %get-tuple-element.180.sin_ref, ...), custom_call_target="tpu_custom_call" | custom-call | flops 1 | bytes 1 | tf_op jit(solution)/shard_map/qkv/pallas_call | solution.py:168
  115.3 3.2 %collective-permute-start.20 = (bf16[128,3072]{1,0:T(8,128)(2,1)}, bf16[128,3072]{1,0:T(8,128)(2,1)S(1)}, u32[]{:S(2)}, u32[]{:S(2)}) collective-permute-start(bf16[128,3072]{1,0:T(8,128)(2,1)} %bitcast.16.refs_4_), channel_id=1, source_target_pairs={{0,6},{1,7},{2,0},{3,1},{4,2},{5,3},{6,4},{7,5},{8,14},{9,15},{10,... | collective-permute-start | bytes 2359304 | tf_op jit(solution)/shard_map/ppermute | solution.py:37
  118.6 2.7 %collective-permute-done.17.refs_6_ = bf16[1024,256]{1,0:T(8,128)(2,1)S(1)} collective-permute-done((bf16[1024,256]{1,0:T(8,128)(2,1)S(1)}, bf16[1024,256]{1,0:T(8,128)(2,1)S(1)}, u32[]{:S(2)}, u32[]{:S(2)}) %collective-permute-start.17) | collective-permute-done | bytes 524320 | tf_op jit(solution)/shard_map/ppermute | solution.py:406
  121.5 9.4 %collective-permute-start.22 = (bf16[1024,256]{1,0:T(8,128)(2,1)S(1)}, bf16[1024,256]{1,0:T(8,128)(2,1)S(1)}, u32[]{:S(2)}, u32[]{:S(2)}) collective-permute-start(bf16[1024,256]{1,0:T(8,128)(2,1)S(1)} %pad_maximum_fusion.1.refs_5_), channel_id=1, source_target_pairs={{16,0},{32,16},{48,32},{64,48},{80,64},{96,80},{112,96},{128,112},... | collective-permute-start | bytes 1572872 | tf_op jit(solution)/shard_map/ppermute | solution.py:406
  130.8 5.8 %collective-permute-done.19.refs_6_ = bf16[128,3072]{1,0:T(8,128)(2,1)S(1)} collective-permute-done((bf16[128,3072]{1,0:T(8,128)(2,1)}, bf16[128,3072]{1,0:T(8,128)(2,1)S(1)}, u32[]{:S(2)}, u32[]{:S(2)}) %collective-permute-start.19) | collective-permute-done | bytes 786464 | tf_op jit(solution)/shard_map/ppermute | solution.py:37
  138.2 3.9 %collective-permute-done.21.refs_7_ = bf16[1024,256]{1,0:T(8,128)(2,1)S(1)} collective-permute-done((bf16[1024,256]{1,0:T(8,128)(2,1)S(1)}, bf16[1024,256]{1,0:T(8,128)(2,1)S(1)}, u32[]{:S(2)}, u32[]{:S(2)}) %collective-permute-start.21) | collective-permute-done | bytes 524320 | tf_op jit(solution)/shard_map/ppermute | solution.py:406
  143.5 2.0 collective-permute-start.24
  145.5 3.7 %collective-permute-start.30 = (bf16[64,3072]{1,0:T(8,128)(2,1)}, bf16[64,3072]{1,0:T(8,128)(2,1)}, u32[]{:S(2)}, u32[]{:S(2)}) collective-permute-start(bf16[64,3072]{1,0:T(8,128)(2,1)} %slice.95), channel_id=1, source_target_pairs={{0,6},{1,7},{2,0},{3,1},{4,2},{5,3},{6,4},{7,5},{8,14},{9,15},{10,... | collective-permute-start | bytes 1179656 | tf_op jit(solution)/shard_map/ppermute | solution.py:37
  149.8 20.7 %attend.1 = (bf16[1024,128]{1,0:T(8,128)(2,1)}, bf16[1024,128]{1,0:T(8,128)(2,1)}) custom-call(s32[2]{0:T(128)} %add_convert_fusion.2.flag_ref, bf16[512,128]{1,0:T(8,128)(2,1)} %get-tuple-element.110.refs_0_, bf16[512,384]{1,0:T(8,128)(2,1)} %copy-done.12, bf16[512,128]{1,0:T(8,128)(2,1)} %copy-done.3, bf16[512,384]{1,0:T(8,128)(2,1)} %copy-done.13, ...), custom_call_target="tpu_custom_call" | custom-call | flops 1 | bytes 1 | tf_op jit(solution)/shard_map/attend/pallas_call | solution.py:236
  170.5 3.2 %collective-permute-start.25 = (bf16[1024,128]{1,0:T(8,128)(2,1)}, bf16[1024,128]{1,0:T(8,128)(2,1)}, u32[]{:S(2)}, u32[]{:S(2)}) collective-permute-start(bf16[1024,128]{1,0:T(8,128)(2,1)} %get-tuple-element.138), channel_id=1, source_target_pairs={{0,8},{1,9},{2,10},{3,11},{4,12},{5,13},{6,14},{7,15},{8,0},{9,1},... | collective-permute-start | bytes 786440 | tf_op jit(solution)/shard_map/ppermute | solution.py:37
  173.8 1.8 slice.96
  175.5 1.8 slice.97
  177.3 3.2 %collective-permute-start.32 = (bf16[64,3072]{1,0:T(8,128)(2,1)}, bf16[64,3072]{1,0:T(8,128)(2,1)}, u32[]{:S(2)}, u32[]{:S(2)}) collective-permute-start(bf16[64,3072]{1,0:T(8,128)(2,1)} %slice.97), channel_id=1, source_target_pairs={{0,6},{1,7},{2,0},{3,1},{4,2},{5,3},{6,4},{7,5},{8,14},{9,15},{10,... | collective-permute-start | bytes 1179656 | tf_op jit(solution)/shard_map/ppermute | solution.py:37
  180.6 4.5 %collective-permute-done.25.far_ref = bf16[1024,128]{1,0:T(8,128)(2,1)} collective-permute-done((bf16[1024,128]{1,0:T(8,128)(2,1)}, bf16[1024,128]{1,0:T(8,128)(2,1)}, u32[]{:S(2)}, u32[]{:S(2)}) %collective-permute-start.25) | collective-permute-done | bytes 262176 | tf_op jit(solution)/shard_map/ppermute | solution.py:37
  185.1 1.9 pair_heads.1
  187.0 3.2 %collective-permute-start.27 = (bf16[256,256]{1,0:T(8,128)(2,1)}, bf16[256,256]{1,0:T(8,128)(2,1)S(1)}, u32[]{:S(2)}, u32[]{:S(2)}) collective-permute-start(bf16[256,256]{1,0:T(8,128)(2,1)} %get-tuple-element.141), channel_id=1, source_target_pairs={{0,6},{1,7},{2,0},{3,1},{4,2},{5,3},{6,4},{7,5},{8,14},{9,15},{10,... | collective-permute-start | bytes 393224 | tf_op jit(solution)/shard_map/ppermute | solution.py:37
  190.2 3.4 %collective-permute-done.26.refs_1_ = bf16[256,256]{1,0:T(8,128)(2,1)S(1)} collective-permute-done((bf16[256,256]{1,0:T(8,128)(2,1)}, bf16[256,256]{1,0:T(8,128)(2,1)S(1)}, u32[]{:S(2)}, u32[]{:S(2)}) %collective-permute-start.26) | collective-permute-done | bytes 131104 | tf_op jit(solution)/shard_map/ppermute | solution.py:37
  193.6 2.2 collective-permute-done.27.refs_2_
  197.5 7.3 %out_project.1 = (f32[128,3072]{1,0:T(8,128)}, bf16[128,3072]{1,0:T(8,128)(2,1)}) custom-call(bf16[256,256]{1,0:T(8,128)(2,1)} %get-tuple-element.139.refs_0_, bf16[256,256]{1,0:T(8,128)(2,1)} %copy-done.20, bf16[256,256]{1,0:T(8,128)(2,1)} %copy-done.21, bf16[256,256]{1,0:T(8,128)(2,1)} %copy-done.22, bf16[128,3072]{1,0:T(8,128)(2,1)} %bitcast.16.refs_4_, ...), custom_call_target="tpu_custom_call" | custom-call | flops 1 | bytes 1 | tf_op jit(solution)/shard_map/out_project/pallas_call | solution.py:289
  204.9 2.6 %collective-permute-done.33.got_ref = bf16[128,3072]{1,0:T(8,128)(2,1)} collective-permute-done((bf16[128,3072]{1,0:T(8,128)(2,1)}, bf16[128,3072]{1,0:T(8,128)(2,1)}, u32[]{:S(2)}, u32[]{:S(2)}) %collective-permute-start.33) | collective-permute-done | bytes 786464 | tf_op jit(solution)/shard_map/ppermute | solution.py:37
  207.5 3.9 %finish.1 = (bf16[128,3072]{1,0:T(8,128)(2,1)}, bf16[128,768]{1,0:T(8,128)(2,1)}, bf16[128,768]{1,0:T(8,128)(2,1)}, bf16[128,768]{1,0:T(8,128)(2,1)}, bf16[128,768]{1,0:T(8,128)(2,1)}) custom-call(bf16[128,3072]{1,0:T(8,128)(2,1)} %bitcast.48, f32[1,3072]{1,0:T(1,128)} %get-tuple-element.165.gate_ref, f32[128,3072]{1,0:T(8,128)} %get-tuple-element.147.mine_ref, ...), custom_call_target="tpu_custom_call" | custom-call | flops 1 | bytes 1 | tf_op jit(solution)/shard_map/finish/pallas_call | solution.py:328
  215.4 1.9 collective-permute-start.34
  223.8 5.1 %collective-permute-done.40 = bf16[128,192]{1,0:T(8,128)(2,1)} collective-permute-done((bf16[128,192]{1,0:T(8,128)(2,1)}, bf16[128,192]{1,0:T(8,128)(2,1)}, u32[]{:S(2)}, u32[]{:S(2)}) %collective-permute-start.40) | collective-permute-done | bytes 49184 | tf_op jit(solution)/shard_map/ppermute | solution.py:454
  228.9 1.6 fusion.4
  232.1 8.4 %collective-permute-done.34 = bf16[128,3072]{1,0:T(8,128)(2,1)} collective-permute-done((bf16[128,3072]{1,0:T(8,128)(2,1)}, bf16[128,3072]{1,0:T(8,128)(2,1)}, u32[]{:S(2)}, u32[]{:S(2)}) %collective-permute-start.34) | collective-permute-done | bytes 786464 | tf_op jit(solution)/shard_map/ppermute | solution.py:445
  240.6 2.1 select_bitcast_fusion
  (158 shorter events, 38.6 us)
Async XLA Ops:
  3.2 23.8 %collective-permute-start.1 = (bf16[128,3072]{1,0:T(8,128)(2,1)}, bf16[128,3072]{1,0:T(8,128)(2,1)}, u32[]{:S(2)}, u32[]{:S(2)}) collective-permute-start(bf16[128,3072]{1,0:T(8,128)(2,1)} %norm_rows.1.refs_0_), channel_id=1, source_target_pairs={{0,2},{1,3},{2,4},{3,5},{4,6},{5,7},{6,0},{7,1},{8,10},{9,11},{10,... | collective-permute-start | bytes 2359304 | tf_op jit(solution)/shard_map/ppermute | solution.py:37
  4.7 22.3 %collective-permute-start.2 = (bf16[128,3072]{1,0:T(8,128)(2,1)}, bf16[128,3072]{1,0:T(8,128)(2,1)}, u32[]{:S(2)}, u32[]{:S(2)}) collective-permute-start(bf16[128,3072]{1,0:T(8,128)(2,1)} %norm_rows.1.refs_0_), channel_id=1, source_target_pairs={{0,6},{1,7},{2,0},{3,1},{4,2},{5,3},{6,4},{7,5},{8,14},{9,15},{10,... | collective-permute-start | bytes 2359304 | tf_op jit(solution)/shard_map/ppermute | solution.py:37
  6.5 39.9 %collective-permute-start.7 = (bf16[128,3072]{1,0:T(8,128)(2,1)}, bf16[128,3072]{1,0:T(8,128)(2,1)}, u32[]{:S(2)}, u32[]{:S(2)}) collective-permute-start(bf16[128,3072]{1,0:T(8,128)(2,1)} %norm_rows.1.refs_0_), channel_id=1, source_target_pairs={{0,8},{1,9},{2,10},{3,11},{4,12},{5,13},{6,14},{7,15},{8,0},{9,1},... | collective-permute-start | bytes 2359304 | tf_op jit(solution)/shard_map/ppermute | solution.py:37
  11.9 30.7 %collective-permute-start.5 = (bf16[3072,384]{1,0:T(8,128)(2,1)}, bf16[3072,384]{1,0:T(8,128)(2,1)}, u32[]{:S(2)}, u32[]{:S(2)}) collective-permute-start(bf16[3072,384]{1,0:T(8,128)(2,1)} %bitcast.45), channel_id=1, source_target_pairs={{0,1},{1,0},{2,3},{3,2},{4,5},{5,4},{6,7},{7,6},{8,9},{9,8},{10,11... | collective-permute-start | bytes 7077896 | tf_op jit(solution)/shard_map/ppermute | solution.py:37
  16.2 9.6 %collective-permute-start = (f32[1,576]{1,0:T(1,128)}, f32[1,576]{1,0:T(1,128)}, u32[]{:S(2)}, u32[]{:S(2)}) collective-permute-start(f32[1,576]{1,0:T(1,128)} %fusion), channel_id=1, source_target_pairs={{0,1},{1,0},{2,3},{3,2},{4,5},{5,4},{6,7},{7,6},{8,9},{9,8},{10,11... | collective-permute-start | bytes 6920 | tf_op jit(solution)/shard_map/ppermute | solution.py:37
  27.1 5.2 %collective-permute-start.3 = (f32[2,576]{1,0:T(2,128)}, f32[2,576]{1,0:T(2,128)}, u32[]{:S(2)}, u32[]{:S(2)}) collective-permute-start(f32[2,576]{1,0:T(2,128)} %pad_maximum_fusion.6), channel_id=1, source_target_pairs={{0,2},{1,3},{2,0},{3,1},{4,6},{5,7},{6,4},{7,5},{8,10},{9,11},{10,... | collective-permute-start | bytes 13832 | tf_op jit(solution)/shard_map/ppermute | solution.py:37
  33.6 8.2 %collective-permute-start.4 = (f32[4,576]{1,0:T(4,128)}, f32[4,576]{1,0:T(4,128)}, u32[]{:S(2)}, u32[]{:S(2)}) collective-permute-start(f32[4,576]{1,0:T(4,128)} %pad_maximum_fusion.5), channel_id=1, source_target_pairs={{0,4},{1,5},{2,6},{3,7},{4,0},{5,1},{6,2},{7,3},{8,12},{9,13},{10,... | collective-permute-start | bytes 27656 | tf_op jit(solution)/shard_map/ppermute | solution.py:37
  36.3 12.1 %collective-permute-start.8 = (bf16[64,3072]{1,0:T(8,128)(2,1)}, bf16[64,3072]{1,0:T(8,128)(2,1)}, u32[]{:S(2)}, u32[]{:S(2)}) collective-permute-start(bf16[64,3072]{1,0:T(8,128)(2,1)} %slice.77), channel_id=1, source_target_pairs={{0,2},{1,3},{2,4},{3,5},{4,6},{5,7},{6,0},{7,1},{8,10},{9,11},{10,... | collective-permute-start | bytes 1179656 | tf_op jit(solution)/shard_map/ppermute | solution.py:37
  36.5 11.8 %collective-permute-start.9 = (bf16[64,3072]{1,0:T(8,128)(2,1)}, bf16[64,3072]{1,0:T(8,128)(2,1)}, u32[]{:S(2)}, u32[]{:S(2)}) collective-permute-start(bf16[64,3072]{1,0:T(8,128)(2,1)} %slice.78), channel_id=1, source_target_pairs={{0,6},{1,7},{2,0},{3,1},{4,2},{5,3},{6,4},{7,5},{8,14},{9,15},{10,... | collective-permute-start | bytes 1179656 | tf_op jit(solution)/shard_map/ppermute | solution.py:37
  48.4 36.6 %collective-permute-start.10 = (bf16[128,3072]{1,0:T(8,128)(2,1)}, bf16[128,3072]{1,0:T(8,128)(2,1)}, u32[]{:S(2)}, u32[]{:S(2)}) collective-permute-start(bf16[128,3072]{1,0:T(8,128)(2,1)} %collective-permute-done.7.refs_0_), channel_id=1, source_target_pairs={{0,2},{1,3},{2,4},{3,5},{4,6},{5,7},{6,0},{7,1},{8,10},{9,11},{10,... | collective-permute-start | bytes 2359304 | tf_op jit(solution)/shard_map/ppermute | solution.py:37
  48.4 36.6 %collective-permute-start.11 = (bf16[128,3072]{1,0:T(8,128)(2,1)}, bf16[128,3072]{1,0:T(8,128)(2,1)}, u32[]{:S(2)}, u32[]{:S(2)}) collective-permute-start(bf16[128,3072]{1,0:T(8,128)(2,1)} %collective-permute-done.7.refs_0_), channel_id=1, source_target_pairs={{0,6},{1,7},{2,0},{3,1},{4,2},{5,3},{6,4},{7,5},{8,14},{9,15},{10,... | collective-permute-start | bytes 2359304 | tf_op jit(solution)/shard_map/ppermute | solution.py:37
  51.6 22.2 %collective-permute-start.6 = (f32[8,576]{1,0:T(8,128)S(1)}, f32[8,576]{1,0:T(8,128)S(1)}, u32[]{:S(2)}, u32[]{:S(2)}) collective-permute-start(f32[8,576]{1,0:T(8,128)S(1)} %pad_maximum_fusion.3), channel_id=1, source_target_pairs={{0,8},{1,9},{2,10},{3,11},{4,12},{5,13},{6,14},{7,15},{8,0},{9,1},... | collective-permute-start | bytes 55304 | tf_op jit(solution)/shard_map/ppermute | solution.py:37
  70.9 37.3 %collective-permute-start.14 = (bf16[128,3072]{1,0:T(8,128)(2,1)}, bf16[128,3072]{1,0:T(8,128)(2,1)}, u32[]{:S(2)}, u32[]{:S(2)}) collective-permute-start(bf16[128,3072]{1,0:T(8,128)(2,1)} %bitcast.16.refs_4_), channel_id=1, source_target_pairs={{0,8},{1,9},{2,10},{3,11},{4,12},{5,13},{6,14},{7,15},{8,0},{9,1},... | collective-permute-start | bytes 2359304 | tf_op jit(solution)/shard_map/ppermute | solution.py:37
  84.9 23.4 %copy-start.1 = (bf16[3072,384]{1,0:T(8,128)(2,1)S(1)}, bf16[3072,384]{1,0:T(8,128)(2,1)}, u32[]{:S(2)}) copy-start(bf16[3072,384]{1,0:T(8,128)(2,1)} %convolution_convert_fusion.1.w_mine) | copy-start | bytes 7077892
  84.9 23.4 %copy-start.4 = (f32[1,3072]{1,0:T(1,128)S(1)}, f32[1,3072]{1,0:T(1,128)}, u32[]{:S(2)}) copy-start(f32[1,3072]{1,0:T(1,128)} %get-tuple-element.163.shift_ref) | copy-start | bytes 36868
  84.9 23.4 %copy-start.5 = (f32[1,3072]{1,0:T(1,128)S(1)}, f32[1,3072]{1,0:T(1,128)}, u32[]{:S(2)}) copy-start(f32[1,3072]{1,0:T(1,128)} %get-tuple-element.164.scale_ref) | copy-start | bytes 36868
  84.9 23.4 %copy-start.6 = (f32[1,128]{1,0:T(1,128)S(1)}, f32[1,128]{1,0:T(1,128)}, u32[]{:S(2)}) copy-start(f32[1,128]{1,0:T(1,128)} %get-tuple-element.95.gk_ref) | copy-start | bytes 1540
  87.2 3.4 %collective-permute-start.12 = (bf16[512,384]{1,0:T(8,128)(2,1)}, bf16[512,384]{1,0:T(8,128)(2,1)S(1)}, u32[]{:S(2)}, u32[]{:S(2)}) collective-permute-start(bf16[512,384]{1,0:T(8,128)(2,1)} %get-tuple-element.111), channel_id=1, source_target_pairs={{0,1},{1,0},{2,3},{3,2},{4,5},{5,4},{6,7},{7,6},{8,9},{9,8},{10,11... | collective-permute-start | bytes 1179656 | tf_op jit(solution)/shard_map/ppermute | solution.py:37
  87.3 20.9 %collective-permute-start.13 = (bf16[64,3072]{1,0:T(8,128)(2,1)S(1)}, bf16[64,3072]{1,0:T(8,128)(2,1)S(1)}, u32[]{:S(2)}, u32[]{:S(2)}) collective-permute-start(bf16[64,3072]{1,0:T(8,128)(2,1)S(1)} %slice.87), channel_id=1, source_target_pairs={{0,2},{1,3},{2,4},{3,5},{4,6},{5,7},{6,0},{7,1},{8,10},{9,11},{10,... | collective-permute-start | bytes 1179656 | tf_op jit(solution)/shard_map/ppermute | solution.py:37
  87.4 20.9 %collective-permute-start.15 = (bf16[64,3072]{1,0:T(8,128)(2,1)S(1)}, bf16[64,3072]{1,0:T(8,128)(2,1)S(1)}, u32[]{:S(2)}, u32[]{:S(2)}) collective-permute-start(bf16[64,3072]{1,0:T(8,128)(2,1)S(1)} %slice.88), channel_id=1, source_target_pairs={{0,6},{1,7},{2,0},{3,1},{4,2},{5,3},{6,4},{7,5},{8,14},{9,15},{10,... | collective-permute-start | bytes 1179656 | tf_op jit(solution)/shard_map/ppermute | solution.py:37
  92.4 29.0 %collective-permute-start.17 = (bf16[1024,256]{1,0:T(8,128)(2,1)S(1)}, bf16[1024,256]{1,0:T(8,128)(2,1)S(1)}, u32[]{:S(2)}, u32[]{:S(2)}) collective-permute-start(bf16[1024,256]{1,0:T(8,128)(2,1)S(1)} %pad_maximum_fusion.refs_4_), channel_id=1, source_target_pairs={{0,16},{16,32},{32,48},{48,64},{64,80},{80,96},{96,112},{112,128},... | collective-permute-start | bytes 1572872 | tf_op jit(solution)/shard_map/ppermute | solution.py:406
  94.1 27.3 %collective-permute-start.18 = (bf16[1024,256]{1,0:T(8,128)(2,1)S(1)}, bf16[1024,256]{1,0:T(8,128)(2,1)S(1)}, u32[]{:S(2)}, u32[]{:S(2)}) collective-permute-start(bf16[1024,256]{1,0:T(8,128)(2,1)S(1)} %pad_maximum_fusion.refs_4_), channel_id=1, source_target_pairs={{16,0},{32,16},{48,32},{64,48},{80,64},{96,80},{112,96},{128,112},... | collective-permute-start | bytes 1572872 | tf_op jit(solution)/shard_map/ppermute | solution.py:406
  115.1 3.4 %collective-permute-start.16 = (bf16[512,384]{1,0:T(8,128)(2,1)S(1)}, bf16[512,384]{1,0:T(8,128)(2,1)S(1)}, u32[]{:S(2)}, u32[]{:S(2)}) collective-permute-start(bf16[512,384]{1,0:T(8,128)(2,1)S(1)} %get-tuple-element.119), channel_id=1, source_target_pairs={{0,1},{1,0},{2,3},{3,2},{4,5},{5,4},{6,7},{7,6},{8,9},{9,8},{10,11... | collective-permute-start | bytes 1179656 | tf_op jit(solution)/shard_map/ppermute | solution.py:37
  115.2 21.4 %collective-permute-start.19 = (bf16[128,3072]{1,0:T(8,128)(2,1)}, bf16[128,3072]{1,0:T(8,128)(2,1)S(1)}, u32[]{:S(2)}, u32[]{:S(2)}) collective-permute-start(bf16[128,3072]{1,0:T(8,128)(2,1)} %bitcast.16.refs_4_), channel_id=1, source_target_pairs={{0,2},{1,3},{2,4},{3,5},{4,6},{5,7},{6,0},{7,1},{8,10},{9,11},{10,... | collective-permute-start | bytes 2359304 | tf_op jit(solution)/shard_map/ppermute | solution.py:37
  115.3 21.3 %collective-permute-start.20 = (bf16[128,3072]{1,0:T(8,128)(2,1)}, bf16[128,3072]{1,0:T(8,128)(2,1)S(1)}, u32[]{:S(2)}, u32[]{:S(2)}) collective-permute-start(bf16[128,3072]{1,0:T(8,128)(2,1)} %bitcast.16.refs_4_), channel_id=1, source_target_pairs={{0,6},{1,7},{2,0},{3,1},{4,2},{5,3},{6,4},{7,5},{8,14},{9,15},{10,... | collective-permute-start | bytes 2359304 | tf_op jit(solution)/shard_map/ppermute | solution.py:37
  118.5 27.0 %copy-start.13 = (bf16[512,384]{1,0:T(8,128)(2,1)}, bf16[512,384]{1,0:T(8,128)(2,1)S(1)}, u32[]{:S(2)}) copy-start(bf16[512,384]{1,0:T(8,128)(2,1)S(1)} %collective-permute-done.16.refs_3_) | copy-start | bytes 1179652
  121.3 24.2 %copy-start.15 = (bf16[1024,256]{1,0:T(8,128)(2,1)}, bf16[1024,256]{1,0:T(8,128)(2,1)S(1)}, u32[]{:S(2)}) copy-start(bf16[1024,256]{1,0:T(8,128)(2,1)S(1)} %collective-permute-done.17.refs_6_) | copy-start | bytes 1572868
  121.4 24.2 %copy-start.16 = (bf16[1024,256]{1,0:T(8,128)(2,1)}, bf16[1024,256]{1,0:T(8,128)(2,1)S(1)}, u32[]{:S(2)}) copy-start(bf16[1024,256]{1,0:T(8,128)(2,1)S(1)} %collective-permute-done.18.refs_8_) | copy-start | bytes 1572868
  121.4 20.8 %collective-permute-start.21 = (bf16[1024,256]{1,0:T(8,128)(2,1)S(1)}, bf16[1024,256]{1,0:T(8,128)(2,1)S(1)}, u32[]{:S(2)}, u32[]{:S(2)}) collective-permute-start(bf16[1024,256]{1,0:T(8,128)(2,1)S(1)} %pad_maximum_fusion.1.refs_5_), channel_id=1, source_target_pairs={{0,16},{16,32},{32,48},{48,64},{64,80},{80,96},{96,112},{112,128},... | collective-permute-start | bytes 1572872 | tf_op jit(solution)/shard_map/ppermute | solution.py:406
  121.5 20.8 %collective-permute-start.22 = (bf16[1024,256]{1,0:T(8,128)(2,1)S(1)}, bf16[1024,256]{1,0:T(8,128)(2,1)S(1)}, u32[]{:S(2)}, u32[]{:S(2)}) collective-permute-start(bf16[1024,256]{1,0:T(8,128)(2,1)S(1)} %pad_maximum_fusion.1.refs_5_), channel_id=1, source_target_pairs={{16,0},{32,16},{48,32},{64,48},{80,64},{96,80},{112,96},{128,112},... | collective-permute-start | bytes 1572872 | tf_op jit(solution)/shard_map/ppermute | solution.py:406
  142.2 31.6 %collective-permute-start.23 = (bf16[128,3072]{1,0:T(8,128)(2,1)}, bf16[128,3072]{1,0:T(8,128)(2,1)}, u32[]{:S(2)}, u32[]{:S(2)}) collective-permute-start(bf16[128,3072]{1,0:T(8,128)(2,1)} %collective-permute-done.14.refs_5_), channel_id=1, source_target_pairs={{0,2},{1,3},{2,4},{3,5},{4,6},{5,7},{6,0},{7,1},{8,10},{9,11},{10,... | collective-permute-start | bytes 2359304 | tf_op jit(solution)/shard_map/ppermute | solution.py:37
  143.5 30.3 %collective-permute-start.24 = (bf16[128,3072]{1,0:T(8,128)(2,1)}, bf16[128,3072]{1,0:T(8,128)(2,1)}, u32[]{:S(2)}, u32[]{:S(2)}) collective-permute-start(bf16[128,3072]{1,0:T(8,128)(2,1)} %collective-permute-done.14.refs_5_), channel_id=1, source_target_pairs={{0,6},{1,7},{2,0},{3,1},{4,2},{5,3},{6,4},{7,5},{8,14},{9,15},{10,... | collective-permute-start | bytes 2359304 | tf_op jit(solution)/shard_map/ppermute | solution.py:37
  145.5 41.5 %collective-permute-start.29 = (bf16[64,3072]{1,0:T(8,128)(2,1)}, bf16[64,3072]{1,0:T(8,128)(2,1)}, u32[]{:S(2)}, u32[]{:S(2)}) collective-permute-start(bf16[64,3072]{1,0:T(8,128)(2,1)} %slice.94), channel_id=1, source_target_pairs={{0,2},{1,3},{2,4},{3,5},{4,6},{5,7},{6,0},{7,1},{8,10},{9,11},{10,... | collective-permute-start | bytes 1179656 | tf_op jit(solution)/shard_map/ppermute | solution.py:37
  145.5 44.7 %collective-permute-start.30 = (bf16[64,3072]{1,0:T(8,128)(2,1)}, bf16[64,3072]{1,0:T(8,128)(2,1)}, u32[]{:S(2)}, u32[]{:S(2)}) collective-permute-start(bf16[64,3072]{1,0:T(8,128)(2,1)} %slice.95), channel_id=1, source_target_pairs={{0,6},{1,7},{2,0},{3,1},{4,2},{5,3},{6,4},{7,5},{8,14},{9,15},{10,... | collective-permute-start | bytes 1179656 | tf_op jit(solution)/shard_map/ppermute | solution.py:37
  170.5 14.5 %collective-permute-start.25 = (bf16[1024,128]{1,0:T(8,128)(2,1)}, bf16[1024,128]{1,0:T(8,128)(2,1)}, u32[]{:S(2)}, u32[]{:S(2)}) collective-permute-start(bf16[1024,128]{1,0:T(8,128)(2,1)} %get-tuple-element.138), channel_id=1, source_target_pairs={{0,8},{1,9},{2,10},{3,11},{4,12},{5,13},{6,14},{7,15},{8,0},{9,1},... | collective-permute-start | bytes 786440 | tf_op jit(solution)/shard_map/ppermute | solution.py:37
  177.3 19.6 %collective-permute-start.31 = (bf16[64,3072]{1,0:T(8,128)(2,1)}, bf16[64,3072]{1,0:T(8,128)(2,1)}, u32[]{:S(2)}, u32[]{:S(2)}) collective-permute-start(bf16[64,3072]{1,0:T(8,128)(2,1)} %slice.96), channel_id=1, source_target_pairs={{0,2},{1,3},{2,4},{3,5},{4,6},{5,7},{6,0},{7,1},{8,10},{9,11},{10,... | collective-permute-start | bytes 1179656 | tf_op jit(solution)/shard_map/ppermute | solution.py:37
  177.3 19.6 %collective-permute-start.32 = (bf16[64,3072]{1,0:T(8,128)(2,1)}, bf16[64,3072]{1,0:T(8,128)(2,1)}, u32[]{:S(2)}, u32[]{:S(2)}) collective-permute-start(bf16[64,3072]{1,0:T(8,128)(2,1)} %slice.97), channel_id=1, source_target_pairs={{0,6},{1,7},{2,0},{3,1},{4,2},{5,3},{6,4},{7,5},{8,14},{9,15},{10,... | collective-permute-start | bytes 1179656 | tf_op jit(solution)/shard_map/ppermute | solution.py:37
  187.0 6.6 %collective-permute-start.26 = (bf16[256,256]{1,0:T(8,128)(2,1)}, bf16[256,256]{1,0:T(8,128)(2,1)S(1)}, u32[]{:S(2)}, u32[]{:S(2)}) collective-permute-start(bf16[256,256]{1,0:T(8,128)(2,1)} %get-tuple-element.140), channel_id=1, source_target_pairs={{0,2},{1,3},{2,4},{3,5},{4,6},{5,7},{6,0},{7,1},{8,10},{9,11},{10,... | collective-permute-start | bytes 393224 | tf_op jit(solution)/shard_map/ppermute | solution.py:37
  187.0 8.8 %collective-permute-start.27 = (bf16[256,256]{1,0:T(8,128)(2,1)}, bf16[256,256]{1,0:T(8,128)(2,1)S(1)}, u32[]{:S(2)}, u32[]{:S(2)}) collective-permute-start(bf16[256,256]{1,0:T(8,128)(2,1)} %get-tuple-element.141), channel_id=1, source_target_pairs={{0,6},{1,7},{2,0},{3,1},{4,2},{5,3},{6,4},{7,5},{8,14},{9,15},{10,... | collective-permute-start | bytes 393224 | tf_op jit(solution)/shard_map/ppermute | solution.py:37
  190.2 6.7 %collective-permute-start.28 = (bf16[256,256]{1,0:T(8,128)(2,1)}, bf16[256,256]{1,0:T(8,128)(2,1)S(1)}, u32[]{:S(2)}, u32[]{:S(2)}) collective-permute-start(bf16[256,256]{1,0:T(8,128)(2,1)} %get-tuple-element.142), channel_id=1, source_target_pairs={{0,4},{1,5},{2,6},{3,7},{4,0},{5,1},{6,2},{7,3},{8,12},{9,13},{10,... | collective-permute-start | bytes 393224 | tf_op jit(solution)/shard_map/ppermute | solution.py:37
  204.8 2.7 %collective-permute-start.33 = (bf16[128,3072]{1,0:T(8,128)(2,1)}, bf16[128,3072]{1,0:T(8,128)(2,1)}, u32[]{:S(2)}, u32[]{:S(2)}) collective-permute-start(bf16[128,3072]{1,0:T(8,128)(2,1)} %get-tuple-element.148), channel_id=1, source_target_pairs={{0,1},{1,0},{2,3},{3,2},{4,5},{5,4},{6,7},{7,6},{8,9},{9,8},{10,11... | collective-permute-start | bytes 2359304 | tf_op jit(solution)/shard_map/ppermute | solution.py:37
  211.4 5.9 %collective-permute-start.35 = (bf16[128,768]{1,0:T(8,128)(2,1)}, bf16[128,768]{1,0:T(8,128)(2,1)}, u32[]{:S(2)}, u32[]{:S(2)}) collective-permute-start(bf16[128,768]{1,0:T(8,128)(2,1)} %get-tuple-element.151), channel_id=1, source_target_pairs={{240,192},{241,193},{242,194},{243,195},{244,196},{245,197},{246,1... | collective-permute-start | bytes 589832 | tf_op jit(solution)/shard_map/ppermute | solution.py:451
  212.8 4.6 %collective-permute-start.36 = (bf16[128,768]{1,0:T(8,128)(2,1)}, bf16[128,768]{1,0:T(8,128)(2,1)}, u32[]{:S(2)}, u32[]{:S(2)}) collective-permute-start(bf16[128,768]{1,0:T(8,128)(2,1)} %get-tuple-element.152), channel_id=1, source_target_pairs={{240,208},{241,209},{242,210},{243,211},{244,212},{245,213},{246,2... | collective-permute-start | bytes 589832 | tf_op jit(solution)/shard_map/ppermute | solution.py:451
  214.1 3.3 %collective-permute-start.37 = (bf16[128,768]{1,0:T(8,128)(2,1)}, bf16[128,768]{1,0:T(8,128)(2,1)}, u32[]{:S(2)}, u32[]{:S(2)}) collective-permute-start(bf16[128,768]{1,0:T(8,128)(2,1)} %get-tuple-element.153), channel_id=1, source_target_pairs={{240,224},{241,225},{242,226},{243,227},{244,228},{245,229},{246,2... | collective-permute-start | bytes 589832 | tf_op jit(solution)/shard_map/ppermute | solution.py:451
  215.4 25.1 %collective-permute-start.34 = (bf16[128,3072]{1,0:T(8,128)(2,1)}, bf16[128,3072]{1,0:T(8,128)(2,1)}, u32[]{:S(2)}, u32[]{:S(2)}) collective-permute-start(bf16[128,3072]{1,0:T(8,128)(2,1)} %get-tuple-element.149), channel_id=1, source_target_pairs={{0,16},{16,32},{32,48},{48,64},{64,80},{80,96},{96,112},{112,128},... | collective-permute-start | bytes 2359304 | tf_op jit(solution)/shard_map/ppermute | solution.py:445
  219.9 3.8 %collective-permute-start.38 = (bf16[128,192]{1,0:T(8,128)(2,1)}, bf16[128,192]{1,0:T(8,128)(2,1)}, u32[]{:S(2)}, u32[]{:S(2)}) collective-permute-start(bf16[128,192]{1,0:T(8,128)(2,1)} %get-tuple-element.158), channel_id=1, source_target_pairs={{192,0},{208,16},{224,32},{240,48},{193,1},{209,17},{225,33},{241,... | collective-permute-start | bytes 147464 | tf_op jit(solution)/shard_map/ppermute | solution.py:454
  221.2 2.6 %collective-permute-start.39 = (bf16[128,192]{1,0:T(8,128)(2,1)}, bf16[128,192]{1,0:T(8,128)(2,1)}, u32[]{:S(2)}, u32[]{:S(2)}) collective-permute-start(bf16[128,192]{1,0:T(8,128)(2,1)} %get-tuple-element.160), channel_id=1, source_target_pairs={{192,64},{208,80},{224,96},{240,112},{193,65},{209,81},{225,97},{2... | collective-permute-start | bytes 147464 | tf_op jit(solution)/shard_map/ppermute | solution.py:454
  222.5 6.5 %collective-permute-start.40 = (bf16[128,192]{1,0:T(8,128)(2,1)}, bf16[128,192]{1,0:T(8,128)(2,1)}, u32[]{:S(2)}, u32[]{:S(2)}) collective-permute-start(bf16[128,192]{1,0:T(8,128)(2,1)} %get-tuple-element.159), channel_id=1, source_target_pairs={{192,128},{208,144},{224,160},{240,176},{193,129},{209,145},{225,1... | collective-permute-start | bytes 147464 | tf_op jit(solution)/shard_map/ppermute | solution.py:454
  (26 other events, 223.2 us)
where the time goes:
time: 247 us; the launch traced here: 243 us
  starting transfers between devices  83.1 us (34%)
  waiting for transfers between devices  57.1 us (23%)
  Pallas kernels  48.9 us (20%)
  other arithmetic  20.8 us (8%)
  local copies, waits for them, and re-layouts  18.6 us (8%)
  matrix products  11 us (4%)
  between operations  3.34 us (1%)
    ppermute x30, starting transfers between devices, on_seq(): return lax.ppermute(value, 'seq', pairs)  59.7 us
    ppermute x30, waiting for transfers between devices, on_seq(): return lax.ppermute(value, 'seq', pairs)  36.9 us
    pallas_call x1, Pallas kernels, attend(): pl.pallas_call(attend_kernel, in_specs=[SMEM] + [pl.BlockSpec(memory_spac...  20.7 us
    ppermute x4, starting transfers between devices, halo(): return (lax.ppermute(kv, 'segment', up), lax.ppermute(kv, 'segment', down))  13.6 us
    pallas_call x2, Pallas kernels, qkv(): pl.pallas_call(functools.partial(qkv_kernel, len(blocks)), grid=(width //...  12.6 us
    dot_general x2, matrix products, ordered(): jnp.dot(w, order, preferred_element_type=jnp.float32).astype(jnp.bfloat16)  9.36 us
    ppermute x1, waiting for transfers between devices, shards(): arrived = lax.ppermute(finished, 'segment', up[:-1])  8.41 us
    pallas_call x1, Pallas kernels, out_project(): pl.pallas_call(functools.partial(out_kernel, len(w_parts)), grid=(width /...  7.26 us
  transfers between devices with their start and end apart: 41, of which 14 were waited for; matrix products, arithmetic and copies ran while one was open for 18% of the time, Pallas kernels for 14%

commit v1 on v0

--- a/solution.py
+++ b/solution.py
@@ -416,9 +416,8 @@
     z_normed, z_far_top, kv_near, w_far = tie(z_normed, z_far_top, kv_near, w_far)
     far_half = half_frame(LIMIT, (z_normed, z_below, z_above, z_far_top, z_far_low), far_table)
     q_far, kv_far = with_partner(*far_half)
-    kv_far, *halo_near = tie(kv_far, *halo_near)
+    kv_far, w_below, w_above = tie(kv_far, w_below, w_above)
     halo_far = halo(kv_far)
-    kv_far, w_below, w_above = tie(kv_far, w_below, w_above)
     top, low = w_below[:half], w_above[half:]
     top, low, w_far, *halo_far = tie(top, low, w_far, *halo_far)
     near_w = [w_out_own, w_below, w_above, on_seq(top, X_UP), on_seq(low, X_DOWN)]

time: 247 us -> 264 us (1.069)
  waiting for transfers between devices: 57.1 us -> 78.7 us
    ppermute x3, waiting for transfers between devices: 5.15 us -> 27.6 us  [shards(): lax.ppermute(spread[:, row * columns:(row + 1) * columns], 'segment', [(s...]
    ppermute x4, waiting for transfers between devices: 6.71 us -> 21.3 us  [halo(): return (lax.ppermute(kv, 'segment', up), lax.ppermute(kv, 'segment', down))]
    ppermute x1, waiting for transfers between devices: 8.41 us -> 0.01 us  [shards(): arrived = lax.ppermute(finished, 'segment', up[:-1])]
    ppermute x30, waiting for transfers between devices: 36.9 us -> 29.9 us  [on_seq(): return lax.ppermute(value, 'seq', pairs)]
    ppermute x4, starting transfers between devices: 13.6 us -> 8.63 us  [halo(): return (lax.ppermute(kv, 'segment', up), lax.ppermute(kv, 'segment', down))]
    ppermute x1, starting transfers between devices: 1.91 us -> 5.76 us  [shards(): arrived = lax.ppermute(finished, 'segment', up[:-1])]
    unnamed x67 -> x63, local copies, waits for them, and re-layouts: 5.39 us -> 4.65 us
  transfers between devices with their start and end apart: 41 -> 41, of which waited for: 14 -> 11; matrix products, arithmetic and copies ran while one was open for 18% -> 17% of each run, Pallas kernels for 14% -> 14%
where the time goes in v1:
time: 264 us; the launch traced here: 261 us
  starting transfers between devices  80.5 us (30%)
  waiting for transfers between devices  78.7 us (30%)
  Pallas kernels  48.9 us (19%)
  other arithmetic  20.6 us (8%)
  local copies, waits for them, and re-layouts  17.8 us (7%)
  matrix products  11 us (4%)
  between operations  3.29 us (1%)
    ppermute x30, starting transfers between devices, on_seq(): return lax.ppermute(value, 'seq', pairs)  58.3 us
    ppermute x30, waiting for transfers between devices, on_seq(): return lax.ppermute(value, 'seq', pairs)  29.9 us
    ppermute x3, waiting for transfers between devices, shards(): lax.ppermute(spread[:, row * columns:(row + 1) * columns], 'segment', [(s...  27.6 us
    ppermute x4, waiting for transfers between devices, halo(): return (lax.ppermute(kv, 'segment', up), lax.ppermute(kv, 'segment', down))  21.3 us
    pallas_call x1, Pallas kernels, attend(): pl.pallas_call(attend_kernel, in_specs=[SMEM] + [pl.BlockSpec(memory_spac...  20.7 us
    pallas_call x2, Pallas kernels, qkv(): pl.pallas_call(functools.partial(qkv_kernel, len(blocks)), grid=(width //...  12.6 us
    dot_general x2, matrix products, ordered(): jnp.dot(w, order, preferred_element_type=jnp.float32).astype(jnp.bfloat16)  9.36 us
    ppermute x4, starting transfers between devices, halo(): return (lax.ppermute(kv, 'segment', up), lax.ppermute(kv, 'segment', down))  8.63 us
  transfers between devices with their start and end apart: 41, of which 11 were waited for; matrix products, arithmetic and copies ran while one was open for 17% of the time, Pallas kernels for 14%

profile of v1, /device:TPU:64, one launch (start us, length us, event | category | flops | bytes accessed | tf_op | source)
XLA Modules:
  0.0 260.7 jit_solution(17789478304433122325)
XLA Ops:
  0.7 2.6 norm_rows.1.refs_0_
  3.2 1.5 collective-permute-start.1
  4.7 1.7 collective-permute-start.2
  6.5 5.4 %collective-permute-start.7 = (bf16[128,3072]{1,0:T(8,128)(2,1)}, bf16[128,3072]{1,0:T(8,128)(2,1)}, u32[]{:S(2)}, u32[]{:S(2)}) collective-permute-start(bf16[128,3072]{1,0:T(8,128)(2,1)} %norm_rows.1.refs_0_), channel_id=1, source_target_pairs={{0,8},{1,9},{2,10},{3,11},{4,12},{5,13},{6,14},{7,15},{8,0},{9,1},... | collective-permute-start | bytes 2359304 | tf_op jit(solution)/shard_map/ppermute | solution.py:37
  14.5 1.6 fusion
  20.3 4.7 %convolution_convert_fusion.1.w_mine = bf16[3072,384]{1,0:T(8,128)(2,1)} fusion(bf16[3072,384]{1,0:T(8,128)(2,1)} %bitcast.46, bf16[384,384]{1,0:T(8,128)(2,1)} %constant.127.clone), kind=kOutput, calls=%fused_computation.1 | convolution fusion | flops 907149312 | bytes 5013504 | tf_op jit(solution)/shard_map/dot_general | solution.py:354
  28.6 1.8 slice.77
  30.3 1.8 slice.78
  33.4 2.7 %collective-permute-start.4 = (f32[4,576]{1,0:T(4,128)}, f32[4,576]{1,0:T(4,128)}, u32[]{:S(2)}, u32[]{:S(2)}) collective-permute-start(f32[4,576]{1,0:T(4,128)} %pad_maximum_fusion.5), channel_id=1, source_target_pairs={{0,4},{1,5},{2,6},{3,7},{4,0},{5,1},{6,2},{7,3},{8,12},{9,13},{10,... | collective-permute-start | bytes 27656 | tf_op jit(solution)/shard_map/ppermute | solution.py:37
  36.4 3.0 %collective-permute-start.9 = (bf16[64,3072]{1,0:T(8,128)(2,1)}, bf16[64,3072]{1,0:T(8,128)(2,1)}, u32[]{:S(2)}, u32[]{:S(2)}) collective-permute-start(bf16[64,3072]{1,0:T(8,128)(2,1)} %slice.78), channel_id=1, source_target_pairs={{0,6},{1,7},{2,0},{3,1},{4,2},{5,3},{6,4},{7,5},{8,14},{9,15},{10,... | collective-permute-start | bytes 1179656 | tf_op jit(solution)/shard_map/ppermute | solution.py:37
  40.0 1.6 bitcast_select_fusion.1
  42.4 3.9 %collective-permute-done.7.refs_0_ = bf16[128,3072]{1,0:T(8,128)(2,1)} collective-permute-done((bf16[128,3072]{1,0:T(8,128)(2,1)}, bf16[128,3072]{1,0:T(8,128)(2,1)}, u32[]{:S(2)}, u32[]{:S(2)}) %collective-permute-start.7) | collective-permute-done | bytes 786464 | tf_op jit(solution)/shard_map/ppermute | solution.py:37
  46.3 1.9 collective-permute-done.8.refs_3_
  48.2 3.2 %collective-permute-start.11 = (bf16[128,3072]{1,0:T(8,128)(2,1)}, bf16[128,3072]{1,0:T(8,128)(2,1)}, u32[]{:S(2)}, u32[]{:S(2)}) collective-permute-start(bf16[128,3072]{1,0:T(8,128)(2,1)} %collective-permute-done.7.refs_0_), channel_id=1, source_target_pairs={{0,6},{1,7},{2,0},{3,1},{4,2},{5,3},{6,4},{7,5},{8,14},{9,15},{10,... | collective-permute-start | bytes 2359304 | tf_op jit(solution)/shard_map/ppermute | solution.py:37
  51.5 14.8 %collective-permute-start.6 = (f32[8,576]{1,0:T(8,128)S(1)}, f32[8,576]{1,0:T(8,128)S(1)}, u32[]{:S(2)}, u32[]{:S(2)}) collective-permute-start(f32[8,576]{1,0:T(8,128)S(1)} %pad_maximum_fusion.3), channel_id=1, source_target_pairs={{0,8},{1,9},{2,10},{3,11},{4,12},{5,13},{6,14},{7,15},{8,0},{9,1},... | collective-permute-start | bytes 55304 | tf_op jit(solution)/shard_map/ppermute | solution.py:37
  66.2 4.7 %convolution_convert_fusion.w_other = bf16[3072,384]{1,0:T(8,128)(2,1)} fusion(bf16[3072,384]{1,0:T(8,128)(2,1)} %collective-permute-done.5, bf16[384,384]{1,0:T(8,128)(2,1)} %constant.127.clone), kind=kOutput, calls=%fused_computation | convolution fusion | flops 907149312 | bytes 5013504 | tf_op jit(solution)/shard_map/dot_general | solution.py:354
  70.9 2.7 %collective-permute-start.14 = (bf16[128,3072]{1,0:T(8,128)(2,1)}, bf16[128,3072]{1,0:T(8,128)(2,1)}, u32[]{:S(2)}, u32[]{:S(2)}) collective-permute-start(bf16[128,3072]{1,0:T(8,128)(2,1)} %bitcast.16.refs_4_), channel_id=1, source_target_pairs={{0,8},{1,9},{2,10},{3,11},{4,12},{5,13},{6,14},{7,15},{8,0},{9,1},... | collective-permute-start | bytes 2359304 | tf_op jit(solution)/shard_map/ppermute | solution.py:37
  74.3 1.5 reshape.361
  77.2 7.5 %qkv.2 = (bf16[512,128]{1,0:T(8,128)(2,1)}, bf16[512,256]{1,0:T(8,128)(2,1)}, bf16[512,384]{1,0:T(8,128)(2,1)}) custom-call(f32[1,3072]{1,0:T(1,128)} %get-tuple-element.158.scale_ref, f32[1,3072]{1,0:T(1,128)} %get-tuple-element.157.shift_ref, f32[512,128]{1,0:T(8,128)} %get-tuple-element.89.cos_ref, f32[512,128]{1,0:T(8,128)} %get-tuple-element.90.sin_ref, ...), custom_call_target="tpu_custom_call" | custom-call | flops 1 | bytes 1 | tf_op jit(solution)/shard_map/qkv/pallas_call | solution.py:168
  87.2 3.2 %collective-permute-start.15 = (bf16[64,3072]{1,0:T(8,128)(2,1)S(1)}, bf16[64,3072]{1,0:T(8,128)(2,1)S(1)}, u32[]{:S(2)}, u32[]{:S(2)}) collective-permute-start(bf16[64,3072]{1,0:T(8,128)(2,1)S(1)} %slice.88), channel_id=1, source_target_pairs={{0,6},{1,7},{2,0},{3,1},{4,2},{5,3},{6,4},{7,5},{8,14},{9,15},{10,... | collective-permute-start | bytes 1179656 | tf_op jit(solution)/shard_map/ppermute | solution.py:37
  90.5 3.2 %collective-permute-start.18 = (bf16[128,3072]{1,0:T(8,128)(2,1)}, bf16[128,3072]{1,0:T(8,128)(2,1)S(1)}, u32[]{:S(2)}, u32[]{:S(2)}) collective-permute-start(bf16[128,3072]{1,0:T(8,128)(2,1)} %bitcast.16.refs_4_), channel_id=1, source_target_pairs={{0,6},{1,7},{2,0},{3,1},{4,2},{5,3},{6,4},{7,5},{8,14},{9,15},{10,... | collective-permute-start | bytes 2359304 | tf_op jit(solution)/shard_map/ppermute | solution.py:37
  94.8 13.3 %collective-permute-done.14.refs_5_ = bf16[128,3072]{1,0:T(8,128)(2,1)} collective-permute-done((bf16[128,3072]{1,0:T(8,128)(2,1)}, bf16[128,3072]{1,0:T(8,128)(2,1)}, u32[]{:S(2)}, u32[]{:S(2)}) %collective-permute-start.14) | collective-permute-done | bytes 786464 | tf_op jit(solution)/shard_map/ppermute | solution.py:37
  108.2 1.7 copy-done.2
  109.9 5.1 %qkv.3 = (bf16[512,128]{1,0:T(8,128)(2,1)S(1)}, bf16[512,256]{1,0:T(8,128)(2,1)S(1)}, bf16[512,384]{1,0:T(8,128)(2,1)S(1)}) custom-call(f32[1,3072]{1,0:T(1,128)S(1)} %copy-done.5, f32[1,3072]{1,0:T(1,128)S(1)} %copy-done.4, f32[512,128]{1,0:T(8,128)S(1)} %get-tuple-element.175.cos_ref, f32[512,128]{1,0:T(8,128)S(1)} %get-tuple-element.174.sin_ref, ...), custom_call_target="tpu_custom_call" | custom-call | flops 1 | bytes 1 | tf_op jit(solution)/shard_map/qkv/pallas_call | solution.py:168
  115.0 1.7 collective-permute-done.16.refs_3_
  116.9 1.7 collective-permute-start.20
  118.5 2.7 %collective-permute-start.21 = (bf16[1024,256]{1,0:T(8,128)(2,1)S(1)}, bf16[1024,256]{1,0:T(8,128)(2,1)S(1)}, u32[]{:S(2)}, u32[]{:S(2)}) collective-permute-start(bf16[1024,256]{1,0:T(8,128)(2,1)S(1)} %pad_maximum_fusion.1.refs_5_), channel_id=1, source_target_pairs={{16,0},{32,16},{48,32},{64,48},{80,64},{96,80},{112,96},{128,112},... | collective-permute-start | bytes 1572872 | tf_op jit(solution)/shard_map/ppermute | solution.py:406
  122.8 10.2 %collective-permute-done.20.refs_7_ = bf16[1024,256]{1,0:T(8,128)(2,1)S(1)} collective-permute-done((bf16[1024,256]{1,0:T(8,128)(2,1)S(1)}, bf16[1024,256]{1,0:T(8,128)(2,1)S(1)}, u32[]{:S(2)}, u32[]{:S(2)}) %collective-permute-start.20) | collective-permute-done | bytes 524320 | tf_op jit(solution)/shard_map/ppermute | solution.py:406
  133.2 3.2 %collective-permute-start.24 = (bf16[128,3072]{1,0:T(8,128)(2,1)}, bf16[128,3072]{1,0:T(8,128)(2,1)}, u32[]{:S(2)}, u32[]{:S(2)}) collective-permute-start(bf16[128,3072]{1,0:T(8,128)(2,1)} %collective-permute-done.14.refs_5_), channel_id=1, source_target_pairs={{0,6},{1,7},{2,0},{3,1},{4,2},{5,3},{6,4},{7,5},{8,14},{9,15},{10,... | collective-permute-start | bytes 2359304 | tf_op jit(solution)/shard_map/ppermute | solution.py:37
  137.1 3.6 %collective-permute-start.22 = (bf16[1024,256]{1,0:T(8,128)(2,1)}, bf16[1024,256]{1,0:T(8,128)(2,1)}, u32[]{:S(2)}, u32[]{:S(2)}) collective-permute-start(bf16[1024,256]{1,0:T(8,128)(2,1)} %pad_maximum_fusion.refs_4_), channel_id=1, source_target_pairs={{16,0},{32,16},{48,32},{64,48},{80,64},{96,80},{112,96},{128,112},... | collective-permute-start | bytes 1572872 | tf_op jit(solution)/shard_map/ppermute | solution.py:406
  140.7 11.1 %collective-permute-done.19.refs_6_ = bf16[1024,256]{1,0:T(8,128)(2,1)} collective-permute-done((bf16[1024,256]{1,0:T(8,128)(2,1)}, bf16[1024,256]{1,0:T(8,128)(2,1)}, u32[]{:S(2)}, u32[]{:S(2)}) %collective-permute-start.19) | collective-permute-done | bytes 524320 | tf_op jit(solution)/shard_map/ppermute | solution.py:406
  153.1 20.7 %attend.1 = (bf16[1024,128]{1,0:T(8,128)(2,1)}, bf16[1024,128]{1,0:T(8,128)(2,1)}) custom-call(s32[2]{0:T(128)} %add_convert_fusion.2.flag_ref, bf16[512,128]{1,0:T(8,128)(2,1)} %get-tuple-element.107.refs_0_, bf16[512,384]{1,0:T(8,128)(2,1)} %copy-done.11, bf16[512,128]{1,0:T(8,128)(2,1)} %copy-done.3, bf16[512,384]{1,0:T(8,128)(2,1)} %copy-done.12, ...), custom_call_target="tpu_custom_call" | custom-call | flops 1 | bytes 1 | tf_op jit(solution)/shard_map/attend/pallas_call | solution.py:236
  173.8 3.9 %collective-permute-start.25 = (bf16[1024,128]{1,0:T(8,128)(2,1)}, bf16[1024,128]{1,0:T(8,128)(2,1)}, u32[]{:S(2)}, u32[]{:S(2)}) collective-permute-start(bf16[1024,128]{1,0:T(8,128)(2,1)} %get-tuple-element.132), channel_id=1, source_target_pairs={{0,8},{1,9},{2,10},{3,11},{4,12},{5,13},{6,14},{7,15},{8,0},{9,1},... | collective-permute-start | bytes 786440 | tf_op jit(solution)/shard_map/ppermute | solution.py:37
  177.6 1.8 slice.96
  179.4 1.8 slice.97
  181.2 1.7 collective-permute-start.31
  182.8 1.6 collective-permute-start.32
  185.1 1.9 pair_heads.1
  187.0 2.1 collective-permute-start.26
  191.2 4.3 %collective-permute-done.26.refs_1_ = bf16[256,256]{1,0:T(8,128)(2,1)S(1)} collective-permute-done((bf16[256,256]{1,0:T(8,128)(2,1)}, bf16[256,256]{1,0:T(8,128)(2,1)S(1)}, u32[]{:S(2)}, u32[]{:S(2)}) %collective-permute-start.26) | collective-permute-done | bytes 131104 | tf_op jit(solution)/shard_map/ppermute | solution.py:37
  197.6 7.2 %out_project.1 = (f32[128,3072]{1,0:T(8,128)}, bf16[128,3072]{1,0:T(8,128)(2,1)}) custom-call(bf16[256,256]{1,0:T(8,128)(2,1)} %get-tuple-element.133.refs_0_, bf16[256,256]{1,0:T(8,128)(2,1)} %copy-done.18, bf16[256,256]{1,0:T(8,128)(2,1)} %copy-done.19, bf16[256,256]{1,0:T(8,128)(2,1)} %copy-done.20, bf16[128,3072]{1,0:T(8,128)(2,1)} %bitcast.16.refs_4_, ...), custom_call_target="tpu_custom_call" | custom-call | flops 1 | bytes 1 | tf_op jit(solution)/shard_map/out_project/pallas_call | solution.py:289
  204.9 2.6 %collective-permute-done.33.got_ref = bf16[128,3072]{1,0:T(8,128)(2,1)} collective-permute-done((bf16[128,3072]{1,0:T(8,128)(2,1)}, bf16[128,3072]{1,0:T(8,128)(2,1)}, u32[]{:S(2)}, u32[]{:S(2)}) %collective-permute-start.33) | collective-permute-done | bytes 786464 | tf_op jit(solution)/shard_map/ppermute | solution.py:37
  207.5 3.9 %finish.1 = (bf16[128,3072]{1,0:T(8,128)(2,1)}, bf16[128,768]{1,0:T(8,128)(2,1)}, bf16[128,768]{1,0:T(8,128)(2,1)}, bf16[128,768]{1,0:T(8,128)(2,1)}, bf16[128,768]{1,0:T(8,128)(2,1)}) custom-call(bf16[128,3072]{1,0:T(8,128)(2,1)} %bitcast.48, f32[1,3072]{1,0:T(1,128)} %get-tuple-element.159.gate_ref, f32[128,3072]{1,0:T(8,128)} %get-tuple-element.141.mine_ref, ...), custom_call_target="tpu_custom_call" | custom-call | flops 1 | bytes 1 | tf_op jit(solution)/shard_map/finish/pallas_call | solution.py:328
  215.4 5.8 %collective-permute-start.34 = (bf16[128,3072]{1,0:T(8,128)(2,1)}, bf16[128,3072]{1,0:T(8,128)(2,1)}, u32[]{:S(2)}, u32[]{:S(2)}) collective-permute-start(bf16[128,3072]{1,0:T(8,128)(2,1)} %get-tuple-element.143), channel_id=1, source_target_pairs={{0,16},{16,32},{32,48},{48,64},{64,80},{80,96},{96,112},{112,128},... | collective-permute-start | bytes 2359304 | tf_op jit(solution)/shard_map/ppermute | solution.py:444
  227.6 27.6 %collective-permute-done.40 = bf16[128,192]{1,0:T(8,128)(2,1)} collective-permute-done((bf16[128,192]{1,0:T(8,128)(2,1)}, bf16[128,192]{1,0:T(8,128)(2,1)}, u32[]{:S(2)}, u32[]{:S(2)}) %collective-permute-start.40) | collective-permute-done | bytes 49184 | tf_op jit(solution)/shard_map/ppermute | solution.py:453
  255.2 1.7 fusion.4
  256.9 1.6 copy.17
  258.4 2.1 select_bitcast_fusion
  (154 shorter events, 36.2 us)
Async XLA Ops:
  0.7 17.4 %copy-start.24 = (f32[128]{0:T(128)S(1)}, f32[128]{0:T(128)}, u32[]{:S(2)}) copy-start(f32[128]{0:T(128)} %constant.143) | copy-start | bytes 1540
  3.2 23.7 %collective-permute-start.1 = (bf16[128,3072]{1,0:T(8,128)(2,1)}, bf16[128,3072]{1,0:T(8,128)(2,1)}, u32[]{:S(2)}, u32[]{:S(2)}) collective-permute-start(bf16[128,3072]{1,0:T(8,128)(2,1)} %norm_rows.1.refs_0_), channel_id=1, source_target_pairs={{0,2},{1,3},{2,4},{3,5},{4,6},{5,7},{6,0},{7,1},{8,10},{9,11},{10,... | collective-permute-start | bytes 2359304 | tf_op jit(solution)/shard_map/ppermute | solution.py:37
  4.7 22.2 %collective-permute-start.2 = (bf16[128,3072]{1,0:T(8,128)(2,1)}, bf16[128,3072]{1,0:T(8,128)(2,1)}, u32[]{:S(2)}, u32[]{:S(2)}) collective-permute-start(bf16[128,3072]{1,0:T(8,128)(2,1)} %norm_rows.1.refs_0_), channel_id=1, source_target_pairs={{0,6},{1,7},{2,0},{3,1},{4,2},{5,3},{6,4},{7,5},{8,14},{9,15},{10,... | collective-permute-start | bytes 2359304 | tf_op jit(solution)/shard_map/ppermute | solution.py:37
  6.5 39.9 %collective-permute-start.7 = (bf16[128,3072]{1,0:T(8,128)(2,1)}, bf16[128,3072]{1,0:T(8,128)(2,1)}, u32[]{:S(2)}, u32[]{:S(2)}) collective-permute-start(bf16[128,3072]{1,0:T(8,128)(2,1)} %norm_rows.1.refs_0_), channel_id=1, source_target_pairs={{0,8},{1,9},{2,10},{3,11},{4,12},{5,13},{6,14},{7,15},{8,0},{9,1},... | collective-permute-start | bytes 2359304 | tf_op jit(solution)/shard_map/ppermute | solution.py:37
  11.9 30.5 %collective-permute-start.5 = (bf16[3072,384]{1,0:T(8,128)(2,1)}, bf16[3072,384]{1,0:T(8,128)(2,1)}, u32[]{:S(2)}, u32[]{:S(2)}) collective-permute-start(bf16[3072,384]{1,0:T(8,128)(2,1)} %bitcast.45), channel_id=1, source_target_pairs={{0,1},{1,0},{2,3},{3,2},{4,5},{5,4},{6,7},{7,6},{8,9},{9,8},{10,11... | collective-permute-start | bytes 7077896 | tf_op jit(solution)/shard_map/ppermute | solution.py:37
  16.1 9.6 %collective-permute-start = (f32[1,576]{1,0:T(1,128)}, f32[1,576]{1,0:T(1,128)}, u32[]{:S(2)}, u32[]{:S(2)}) collective-permute-start(f32[1,576]{1,0:T(1,128)} %fusion), channel_id=1, source_target_pairs={{0,1},{1,0},{2,3},{3,2},{4,5},{5,4},{6,7},{7,6},{8,9},{9,8},{10,11... | collective-permute-start | bytes 6920 | tf_op jit(solution)/shard_map/ppermute | solution.py:37
  26.9 5.1 %collective-permute-start.3 = (f32[2,576]{1,0:T(2,128)}, f32[2,576]{1,0:T(2,128)}, u32[]{:S(2)}, u32[]{:S(2)}) collective-permute-start(f32[2,576]{1,0:T(2,128)} %pad_maximum_fusion.6), channel_id=1, source_target_pairs={{0,2},{1,3},{2,0},{3,1},{4,6},{5,7},{6,4},{7,5},{8,10},{9,11},{10,... | collective-permute-start | bytes 13832 | tf_op jit(solution)/shard_map/ppermute | solution.py:37
  33.4 8.3 %collective-permute-start.4 = (f32[4,576]{1,0:T(4,128)}, f32[4,576]{1,0:T(4,128)}, u32[]{:S(2)}, u32[]{:S(2)}) collective-permute-start(f32[4,576]{1,0:T(4,128)} %pad_maximum_fusion.5), channel_id=1, source_target_pairs={{0,4},{1,5},{2,6},{3,7},{4,0},{5,1},{6,2},{7,3},{8,12},{9,13},{10,... | collective-permute-start | bytes 27656 | tf_op jit(solution)/shard_map/ppermute | solution.py:37
  36.1 12.1 %collective-permute-start.8 = (bf16[64,3072]{1,0:T(8,128)(2,1)}, bf16[64,3072]{1,0:T(8,128)(2,1)}, u32[]{:S(2)}, u32[]{:S(2)}) collective-permute-start(bf16[64,3072]{1,0:T(8,128)(2,1)} %slice.77), channel_id=1, source_target_pairs={{0,2},{1,3},{2,4},{3,5},{4,6},{5,7},{6,0},{7,1},{8,10},{9,11},{10,... | collective-permute-start | bytes 1179656 | tf_op jit(solution)/shard_map/ppermute | solution.py:37
  36.4 11.8 %collective-permute-start.9 = (bf16[64,3072]{1,0:T(8,128)(2,1)}, bf16[64,3072]{1,0:T(8,128)(2,1)}, u32[]{:S(2)}, u32[]{:S(2)}) collective-permute-start(bf16[64,3072]{1,0:T(8,128)(2,1)} %slice.78), channel_id=1, source_target_pairs={{0,6},{1,7},{2,0},{3,1},{4,2},{5,3},{6,4},{7,5},{8,14},{9,15},{10,... | collective-permute-start | bytes 1179656 | tf_op jit(solution)/shard_map/ppermute | solution.py:37
  48.2 36.6 %collective-permute-start.10 = (bf16[128,3072]{1,0:T(8,128)(2,1)}, bf16[128,3072]{1,0:T(8,128)(2,1)}, u32[]{:S(2)}, u32[]{:S(2)}) collective-permute-start(bf16[128,3072]{1,0:T(8,128)(2,1)} %collective-permute-done.7.refs_0_), channel_id=1, source_target_pairs={{0,2},{1,3},{2,4},{3,5},{4,6},{5,7},{6,0},{7,1},{8,10},{9,11},{10,... | collective-permute-start | bytes 2359304 | tf_op jit(solution)/shard_map/ppermute | solution.py:37
  48.2 36.6 %collective-permute-start.11 = (bf16[128,3072]{1,0:T(8,128)(2,1)}, bf16[128,3072]{1,0:T(8,128)(2,1)}, u32[]{:S(2)}, u32[]{:S(2)}) collective-permute-start(bf16[128,3072]{1,0:T(8,128)(2,1)} %collective-permute-done.7.refs_0_), channel_id=1, source_target_pairs={{0,6},{1,7},{2,0},{3,1},{4,2},{5,3},{6,4},{7,5},{8,14},{9,15},{10,... | collective-permute-start | bytes 2359304 | tf_op jit(solution)/shard_map/ppermute | solution.py:37
  51.5 22.2 %collective-permute-start.6 = (f32[8,576]{1,0:T(8,128)S(1)}, f32[8,576]{1,0:T(8,128)S(1)}, u32[]{:S(2)}, u32[]{:S(2)}) collective-permute-start(f32[8,576]{1,0:T(8,128)S(1)} %pad_maximum_fusion.3), channel_id=1, source_target_pairs={{0,8},{1,9},{2,10},{3,11},{4,12},{5,13},{6,14},{7,15},{8,0},{9,1},... | collective-permute-start | bytes 55304 | tf_op jit(solution)/shard_map/ppermute | solution.py:37
  70.9 37.2 %collective-permute-start.14 = (bf16[128,3072]{1,0:T(8,128)(2,1)}, bf16[128,3072]{1,0:T(8,128)(2,1)}, u32[]{:S(2)}, u32[]{:S(2)}) collective-permute-start(bf16[128,3072]{1,0:T(8,128)(2,1)} %bitcast.16.refs_4_), channel_id=1, source_target_pairs={{0,8},{1,9},{2,10},{3,11},{4,12},{5,13},{6,14},{7,15},{8,0},{9,1},... | collective-permute-start | bytes 2359304 | tf_op jit(solution)/shard_map/ppermute | solution.py:37
  84.7 23.4 %copy-start.1 = (bf16[3072,384]{1,0:T(8,128)(2,1)S(1)}, bf16[3072,384]{1,0:T(8,128)(2,1)}, u32[]{:S(2)}) copy-start(bf16[3072,384]{1,0:T(8,128)(2,1)} %convolution_convert_fusion.1.w_mine) | copy-start | bytes 7077892
  84.7 23.4 %copy-start.4 = (f32[1,3072]{1,0:T(1,128)S(1)}, f32[1,3072]{1,0:T(1,128)}, u32[]{:S(2)}) copy-start(f32[1,3072]{1,0:T(1,128)} %get-tuple-element.157.shift_ref) | copy-start | bytes 36868
  84.7 23.4 %copy-start.5 = (f32[1,3072]{1,0:T(1,128)S(1)}, f32[1,3072]{1,0:T(1,128)}, u32[]{:S(2)}) copy-start(f32[1,3072]{1,0:T(1,128)} %get-tuple-element.158.scale_ref) | copy-start | bytes 36868
  84.7 23.4 %copy-start.6 = (f32[1,128]{1,0:T(1,128)S(1)}, f32[1,128]{1,0:T(1,128)}, u32[]{:S(2)}) copy-start(f32[1,128]{1,0:T(1,128)} %get-tuple-element.92.gk_ref) | copy-start | bytes 1540
  84.8 23.4 %copy-start.7 = (f32[1,128]{1,0:T(1,128)S(1)}, f32[1,128]{1,0:T(1,128)}, u32[]{:S(2)}) copy-start(f32[1,128]{1,0:T(1,128)} %get-tuple-element.91.gq_ref) | copy-start | bytes 1540
  87.0 3.5 %collective-permute-start.12 = (bf16[512,384]{1,0:T(8,128)(2,1)}, bf16[512,384]{1,0:T(8,128)(2,1)S(1)}, u32[]{:S(2)}, u32[]{:S(2)}) collective-permute-start(bf16[512,384]{1,0:T(8,128)(2,1)} %get-tuple-element.108), channel_id=1, source_target_pairs={{0,1},{1,0},{2,3},{3,2},{4,5},{5,4},{6,7},{7,6},{8,9},{9,8},{10,11... | collective-permute-start | bytes 1179656 | tf_op jit(solution)/shard_map/ppermute | solution.py:37
  87.2 21.0 %collective-permute-start.13 = (bf16[64,3072]{1,0:T(8,128)(2,1)S(1)}, bf16[64,3072]{1,0:T(8,128)(2,1)S(1)}, u32[]{:S(2)}, u32[]{:S(2)}) collective-permute-start(bf16[64,3072]{1,0:T(8,128)(2,1)S(1)} %slice.87), channel_id=1, source_target_pairs={{0,2},{1,3},{2,4},{3,5},{4,6},{5,7},{6,0},{7,1},{8,10},{9,11},{10,... | collective-permute-start | bytes 1179656 | tf_op jit(solution)/shard_map/ppermute | solution.py:37
  87.2 20.9 %collective-permute-start.15 = (bf16[64,3072]{1,0:T(8,128)(2,1)S(1)}, bf16[64,3072]{1,0:T(8,128)(2,1)S(1)}, u32[]{:S(2)}, u32[]{:S(2)}) collective-permute-start(bf16[64,3072]{1,0:T(8,128)(2,1)S(1)} %slice.88), channel_id=1, source_target_pairs={{0,6},{1,7},{2,0},{3,1},{4,2},{5,3},{6,4},{7,5},{8,14},{9,15},{10,... | collective-permute-start | bytes 1179656 | tf_op jit(solution)/shard_map/ppermute | solution.py:37
  90.4 26.4 %collective-permute-start.17 = (bf16[128,3072]{1,0:T(8,128)(2,1)}, bf16[128,3072]{1,0:T(8,128)(2,1)S(1)}, u32[]{:S(2)}, u32[]{:S(2)}) collective-permute-start(bf16[128,3072]{1,0:T(8,128)(2,1)} %bitcast.16.refs_4_), channel_id=1, source_target_pairs={{0,2},{1,3},{2,4},{3,5},{4,6},{5,7},{6,0},{7,1},{8,10},{9,11},{10,... | collective-permute-start | bytes 2359304 | tf_op jit(solution)/shard_map/ppermute | solution.py:37
  90.5 26.4 %collective-permute-start.18 = (bf16[128,3072]{1,0:T(8,128)(2,1)}, bf16[128,3072]{1,0:T(8,128)(2,1)S(1)}, u32[]{:S(2)}, u32[]{:S(2)}) collective-permute-start(bf16[128,3072]{1,0:T(8,128)(2,1)} %bitcast.16.refs_4_), channel_id=1, source_target_pairs={{0,6},{1,7},{2,0},{3,1},{4,2},{5,3},{6,4},{7,5},{8,14},{9,15},{10,... | collective-permute-start | bytes 2359304 | tf_op jit(solution)/shard_map/ppermute | solution.py:37
  114.9 1.8 collective-permute-start.16
  116.8 19.6 %copy-start.12 = (bf16[512,384]{1,0:T(8,128)(2,1)}, bf16[512,384]{1,0:T(8,128)(2,1)S(1)}, u32[]{:S(2)}) copy-start(bf16[512,384]{1,0:T(8,128)(2,1)S(1)} %collective-permute-done.16.refs_3_) | copy-start | bytes 1179652
  116.9 16.2 %collective-permute-start.20 = (bf16[1024,256]{1,0:T(8,128)(2,1)S(1)}, bf16[1024,256]{1,0:T(8,128)(2,1)S(1)}, u32[]{:S(2)}, u32[]{:S(2)}) collective-permute-start(bf16[1024,256]{1,0:T(8,128)(2,1)S(1)} %pad_maximum_fusion.1.refs_5_), channel_id=1, source_target_pairs={{0,16},{16,32},{32,48},{48,64},{64,80},{80,96},{96,112},{112,128},... | collective-permute-start | bytes 1572872 | tf_op jit(solution)/shard_map/ppermute | solution.py:406
  118.5 14.5 %collective-permute-start.21 = (bf16[1024,256]{1,0:T(8,128)(2,1)S(1)}, bf16[1024,256]{1,0:T(8,128)(2,1)S(1)}, u32[]{:S(2)}, u32[]{:S(2)}) collective-permute-start(bf16[1024,256]{1,0:T(8,128)(2,1)S(1)} %pad_maximum_fusion.1.refs_5_), channel_id=1, source_target_pairs={{16,0},{32,16},{48,32},{64,48},{80,64},{96,80},{112,96},{128,112},... | collective-permute-start | bytes 1572872 | tf_op jit(solution)/shard_map/ppermute | solution.py:406
  133.1 44.6 %collective-permute-start.23 = (bf16[128,3072]{1,0:T(8,128)(2,1)}, bf16[128,3072]{1,0:T(8,128)(2,1)}, u32[]{:S(2)}, u32[]{:S(2)}) collective-permute-start(bf16[128,3072]{1,0:T(8,128)(2,1)} %collective-permute-done.14.refs_5_), channel_id=1, source_target_pairs={{0,2},{1,3},{2,4},{3,5},{4,6},{5,7},{6,0},{7,1},{8,10},{9,11},{10,... | collective-permute-start | bytes 2359304 | tf_op jit(solution)/shard_map/ppermute | solution.py:37
  133.2 44.5 %collective-permute-start.24 = (bf16[128,3072]{1,0:T(8,128)(2,1)}, bf16[128,3072]{1,0:T(8,128)(2,1)}, u32[]{:S(2)}, u32[]{:S(2)}) collective-permute-start(bf16[128,3072]{1,0:T(8,128)(2,1)} %collective-permute-done.14.refs_5_), channel_id=1, source_target_pairs={{0,6},{1,7},{2,0},{3,1},{4,2},{5,3},{6,4},{7,5},{8,14},{9,15},{10,... | collective-permute-start | bytes 2359304 | tf_op jit(solution)/shard_map/ppermute | solution.py:37
  136.4 15.3 %collective-permute-start.19 = (bf16[1024,256]{1,0:T(8,128)(2,1)}, bf16[1024,256]{1,0:T(8,128)(2,1)}, u32[]{:S(2)}, u32[]{:S(2)}) collective-permute-start(bf16[1024,256]{1,0:T(8,128)(2,1)} %pad_maximum_fusion.refs_4_), channel_id=1, source_target_pairs={{0,16},{16,32},{32,48},{48,64},{64,80},{80,96},{96,112},{112,128},... | collective-permute-start | bytes 1572872 | tf_op jit(solution)/shard_map/ppermute | solution.py:406
  137.1 16.0 %collective-permute-start.22 = (bf16[1024,256]{1,0:T(8,128)(2,1)}, bf16[1024,256]{1,0:T(8,128)(2,1)}, u32[]{:S(2)}, u32[]{:S(2)}) collective-permute-start(bf16[1024,256]{1,0:T(8,128)(2,1)} %pad_maximum_fusion.refs_4_), channel_id=1, source_target_pairs={{16,0},{32,16},{48,32},{64,48},{80,64},{96,80},{112,96},{128,112},... | collective-permute-start | bytes 1572872 | tf_op jit(solution)/shard_map/ppermute | solution.py:406
  140.7 48.4 %collective-permute-start.29 = (bf16[64,3072]{1,0:T(8,128)(2,1)}, bf16[64,3072]{1,0:T(8,128)(2,1)}, u32[]{:S(2)}, u32[]{:S(2)}) collective-permute-start(bf16[64,3072]{1,0:T(8,128)(2,1)} %slice.94), channel_id=1, source_target_pairs={{0,2},{1,3},{2,4},{3,5},{4,6},{5,7},{6,0},{7,1},{8,10},{9,11},{10,... | collective-permute-start | bytes 1179656 | tf_op jit(solution)/shard_map/ppermute | solution.py:37
  151.7 38.5 %collective-permute-start.30 = (bf16[64,3072]{1,0:T(8,128)(2,1)}, bf16[64,3072]{1,0:T(8,128)(2,1)}, u32[]{:S(2)}, u32[]{:S(2)}) collective-permute-start(bf16[64,3072]{1,0:T(8,128)(2,1)} %slice.95), channel_id=1, source_target_pairs={{0,6},{1,7},{2,0},{3,1},{4,2},{5,3},{6,4},{7,5},{8,14},{9,15},{10,... | collective-permute-start | bytes 1179656 | tf_op jit(solution)/shard_map/ppermute | solution.py:37
  173.8 11.3 %collective-permute-start.25 = (bf16[1024,128]{1,0:T(8,128)(2,1)}, bf16[1024,128]{1,0:T(8,128)(2,1)}, u32[]{:S(2)}, u32[]{:S(2)}) collective-permute-start(bf16[1024,128]{1,0:T(8,128)(2,1)} %get-tuple-element.132), channel_id=1, source_target_pairs={{0,8},{1,9},{2,10},{3,11},{4,12},{5,13},{6,14},{7,15},{8,0},{9,1},... | collective-permute-start | bytes 786440 | tf_op jit(solution)/shard_map/ppermute | solution.py:37
  181.2 15.8 %collective-permute-start.31 = (bf16[64,3072]{1,0:T(8,128)(2,1)}, bf16[64,3072]{1,0:T(8,128)(2,1)}, u32[]{:S(2)}, u32[]{:S(2)}) collective-permute-start(bf16[64,3072]{1,0:T(8,128)(2,1)} %slice.96), channel_id=1, source_target_pairs={{0,2},{1,3},{2,4},{3,5},{4,6},{5,7},{6,0},{7,1},{8,10},{9,11},{10,... | collective-permute-start | bytes 1179656 | tf_op jit(solution)/shard_map/ppermute | solution.py:37
  182.8 14.1 %collective-permute-start.32 = (bf16[64,3072]{1,0:T(8,128)(2,1)}, bf16[64,3072]{1,0:T(8,128)(2,1)}, u32[]{:S(2)}, u32[]{:S(2)}) collective-permute-start(bf16[64,3072]{1,0:T(8,128)(2,1)} %slice.97), channel_id=1, source_target_pairs={{0,6},{1,7},{2,0},{3,1},{4,2},{5,3},{6,4},{7,5},{8,14},{9,15},{10,... | collective-permute-start | bytes 1179656 | tf_op jit(solution)/shard_map/ppermute | solution.py:37
  187.0 8.5 %collective-permute-start.26 = (bf16[256,256]{1,0:T(8,128)(2,1)}, bf16[256,256]{1,0:T(8,128)(2,1)S(1)}, u32[]{:S(2)}, u32[]{:S(2)}) collective-permute-start(bf16[256,256]{1,0:T(8,128)(2,1)} %get-tuple-element.134), channel_id=1, source_target_pairs={{0,2},{1,3},{2,4},{3,5},{4,6},{5,7},{6,0},{7,1},{8,10},{9,11},{10,... | collective-permute-start | bytes 393224 | tf_op jit(solution)/shard_map/ppermute | solution.py:37
  189.1 6.5 %collective-permute-start.27 = (bf16[256,256]{1,0:T(8,128)(2,1)}, bf16[256,256]{1,0:T(8,128)(2,1)S(1)}, u32[]{:S(2)}, u32[]{:S(2)}) collective-permute-start(bf16[256,256]{1,0:T(8,128)(2,1)} %get-tuple-element.135), channel_id=1, source_target_pairs={{0,6},{1,7},{2,0},{3,1},{4,2},{5,3},{6,4},{7,5},{8,14},{9,15},{10,... | collective-permute-start | bytes 393224 | tf_op jit(solution)/shard_map/ppermute | solution.py:37
  190.3 6.7 %collective-permute-start.28 = (bf16[256,256]{1,0:T(8,128)(2,1)}, bf16[256,256]{1,0:T(8,128)(2,1)S(1)}, u32[]{:S(2)}, u32[]{:S(2)}) collective-permute-start(bf16[256,256]{1,0:T(8,128)(2,1)} %get-tuple-element.136), channel_id=1, source_target_pairs={{0,4},{1,5},{2,6},{3,7},{4,0},{5,1},{6,2},{7,3},{8,12},{9,13},{10,... | collective-permute-start | bytes 393224 | tf_op jit(solution)/shard_map/ppermute | solution.py:37
  204.8 2.7 %collective-permute-start.33 = (bf16[128,3072]{1,0:T(8,128)(2,1)}, bf16[128,3072]{1,0:T(8,128)(2,1)}, u32[]{:S(2)}, u32[]{:S(2)}) collective-permute-start(bf16[128,3072]{1,0:T(8,128)(2,1)} %get-tuple-element.142), channel_id=1, source_target_pairs={{0,1},{1,0},{2,3},{3,2},{4,5},{5,4},{6,7},{7,6},{8,9},{9,8},{10,11... | collective-permute-start | bytes 2359304 | tf_op jit(solution)/shard_map/ppermute | solution.py:37
  211.4 9.8 %collective-permute-start.35 = (bf16[128,768]{1,0:T(8,128)(2,1)}, bf16[128,768]{1,0:T(8,128)(2,1)}, u32[]{:S(2)}, u32[]{:S(2)}) collective-permute-start(bf16[128,768]{1,0:T(8,128)(2,1)} %get-tuple-element.145), channel_id=1, source_target_pairs={{240,192},{241,193},{242,194},{243,195},{244,196},{245,197},{246,1... | collective-permute-start | bytes 589832 | tf_op jit(solution)/shard_map/ppermute | solution.py:450
  212.7 8.5 %collective-permute-start.36 = (bf16[128,768]{1,0:T(8,128)(2,1)}, bf16[128,768]{1,0:T(8,128)(2,1)}, u32[]{:S(2)}, u32[]{:S(2)}) collective-permute-start(bf16[128,768]{1,0:T(8,128)(2,1)} %get-tuple-element.146), channel_id=1, source_target_pairs={{240,208},{241,209},{242,210},{243,211},{244,212},{245,213},{246,2... | collective-permute-start | bytes 589832 | tf_op jit(solution)/shard_map/ppermute | solution.py:450
  214.1 7.1 %collective-permute-start.37 = (bf16[128,768]{1,0:T(8,128)(2,1)}, bf16[128,768]{1,0:T(8,128)(2,1)}, u32[]{:S(2)}, u32[]{:S(2)}) collective-permute-start(bf16[128,768]{1,0:T(8,128)(2,1)} %get-tuple-element.147), channel_id=1, source_target_pairs={{240,224},{241,225},{242,226},{243,227},{244,228},{245,229},{246,2... | collective-permute-start | bytes 589832 | tf_op jit(solution)/shard_map/ppermute | solution.py:450
  215.4 43.0 %collective-permute-start.34 = (bf16[128,3072]{1,0:T(8,128)(2,1)}, bf16[128,3072]{1,0:T(8,128)(2,1)}, u32[]{:S(2)}, u32[]{:S(2)}) collective-permute-start(bf16[128,3072]{1,0:T(8,128)(2,1)} %get-tuple-element.143), channel_id=1, source_target_pairs={{0,16},{16,32},{32,48},{48,64},{64,80},{80,96},{96,112},{112,128},... | collective-permute-start | bytes 2359304 | tf_op jit(solution)/shard_map/ppermute | solution.py:444
  223.8 3.8 %collective-permute-start.38 = (bf16[128,192]{1,0:T(8,128)(2,1)}, bf16[128,192]{1,0:T(8,128)(2,1)}, u32[]{:S(2)}, u32[]{:S(2)}) collective-permute-start(bf16[128,192]{1,0:T(8,128)(2,1)} %get-tuple-element.152), channel_id=1, source_target_pairs={{192,0},{208,16},{224,32},{240,48},{193,1},{209,17},{225,33},{241,... | collective-permute-start | bytes 147464 | tf_op jit(solution)/shard_map/ppermute | solution.py:453
  225.1 2.6 collective-permute-start.39
  226.3 28.9 %collective-permute-start.40 = (bf16[128,192]{1,0:T(8,128)(2,1)}, bf16[128,192]{1,0:T(8,128)(2,1)}, u32[]{:S(2)}, u32[]{:S(2)}) collective-permute-start(bf16[128,192]{1,0:T(8,128)(2,1)} %get-tuple-element.153), channel_id=1, source_target_pairs={{192,128},{208,144},{224,160},{240,176},{193,129},{209,145},{225,1... | collective-permute-start | bytes 147464 | tf_op jit(solution)/shard_map/ppermute | solution.py:453
  (24 other events, 210.8 us)
